TPU v7x, 256 devices: a whole 4x4x8 slice. The times are simulated.
256 devices in a mesh: freq: 16 (over x, y), clus: 16 (over z, core).
Axes of the slice: x: 4, y: 4, z: 8, core: 2. Of those that a mesh axis runs over, the one named last changes fastest.
Arguments:
- history: bfloat16 [1024, 8, 2048], P('freq', None, 'clus'), may hold values from -6 to 6
- near_blocks: bfloat16 [16, 4, 512, 2, 128, 128], P('clus', None, 'freq'), may hold values from -0.1875 to 0.1875
- near_list: int32 [16, 4], replicated, may hold values from 0 to 15, as said below
- basis_out: bfloat16 [512, 2, 32, 2048], P('freq', None, None, 'clus'), may hold values from -0.75 to 0.75
- basis_in: bfloat16 [512, 2, 32, 2048], P('freq', None, None, 'clus'), may hold values from -0.375 to 0.375
- coupling: bfloat16 [16, 512, 2, 32, 512], P('clus', 'freq'), may hold values from -0.25 to 0.25
- ranks: int32 [16, 512, 16], P('clus', 'freq'), may hold values from 4 to 32
Outputs:
- potential: bfloat16 [512, 2, 8, 2048], P('freq', None, None, 'clus')
Inputs may be any that keep to these rules, and one draw needn't show every extreme that they name: `near_list`: row t starts with t itself; its other 3 entries are distinct shards other than t, each (t + d) mod 16 for some d with 1 <= |d| <= 3.
All inputs are finite; a program needn't handle non-finite values.
Results may differ from a plain program's by a relative error of at most 0.0055.
Values may be sent and summed in bfloat16 or wider, within the bound.
No kernel may reach another device: no remote copies, remote signals or barrier semaphores. Data moves between devices by JAX's collectives and lax.ppermute only.
A program may use at most 128 MiB of HBM per device.

v0:
```python
import math

import jax
import jax.numpy as jnp
from jax import lax
from jax.sharding import PartitionSpec as P

STEPS = 1024


def from_behind(block, axis, distance):
    devices = range(lax.axis_size(axis))
    route = [((i - distance) % len(devices), i) for i in devices]
    return lax.ppermute(block, axis, route)


def wave_table(count, first_step, length, total):
    waves = lax.iota(jnp.int32, count)
    steps = first_step + lax.iota(jnp.int32, length)
    phase = waves[:, None] * steps[None, :] % total
    angle = phase.astype(jnp.float32) * (2.0 * math.pi / total)
    weight = jnp.exp(steps.astype(jnp.float32) * (-math.log(2.0) / total)) * total ** (-0.5)
    return (weight[None, :] * jnp.cos(angle), -weight[None, :] * jnp.sin(angle))


def transform(history, cos_tab, sin_tab):
    flat = history.reshape(history.shape[0], -1).astype(jnp.float32)
    real_part = jnp.dot(cos_tab, flat, precision=lax.Precision.HIGHEST)
    imag_part = jnp.dot(sin_tab, flat, precision=lax.Precision.HIGHEST)
    return jnp.stack([real_part, imag_part], 1).reshape(
        cos_tab.shape[0], 2, history.shape[1], history.shape[2]
    )


def complex_product(form, left_re, left_im, right_re, right_im):

    def product(left, right):
        return jnp.einsum(form, left, right, preferred_element_type=jnp.float32)

    return (
        product(left_re, right_re) - product(left_im, right_im),
        product(left_re, right_im) + product(left_im, right_re),
    )


def far_mask(limit, nearby, clusters, rank):
    position = lax.iota(jnp.int32, rank)
    keep_out = position[None, None, :] < limit[:, :, None]
    keep_in = keep_out & jnp.logical_not(nearby)[None, :, None]
    mask = jnp.transpose(keep_out, (0, 2, 1))[:, :, :, None] & keep_in[:, None, :, :]
    return mask.reshape(limit.shape[0], rank, clusters * rank)


def local(history, near_blocks, near_list, basis_out, basis_in, coupling, ranks):
    steps_dev, exc, panels = history.shape
    waves_dev = basis_in.shape[0]
    rank = basis_in.shape[2]
    clusters = lax.axis_size("clus")
    first_step = lax.axis_index("freq") * steps_dev
    cos_tab, sin_tab = wave_table(lax.axis_size("freq") * waves_dev, first_step, steps_dev, STEPS)
    dens = lax.psum_scatter(
        transform(history, cos_tab, sin_tab), "freq", scatter_dimension=0, tiled=True
    ).astype(jnp.bfloat16)
    me_index = lax.axis_index("clus")
    mine = lax.dynamic_index_in_dim(near_list, me_index, 0, keepdims=False)
    near_count = near_list.shape[1]
    slot_values = [dens] + [jnp.zeros_like(dens) for slot in range(1, near_count)]
    for distance in range(1, near_count):
        for direction in (1, -1):
            moved = from_behind(dens, "clus", direction * distance)
            anchor = (me_index - direction * distance + clusters) % clusters
            for slot in range(1, near_count):
                slot_values[slot] = jnp.where(mine[slot] == anchor, moved, slot_values[slot])
    sources = jnp.stack(slot_values)
    blocks = near_blocks[0]
    near_re, near_im = complex_product(
        "jkpq,jkeq->kep", blocks[:, :, 0], blocks[:, :, 1], sources[:, :, 0], sources[:, :, 1]
    )
    coeff_re, coeff_im = complex_product(
        "krp,kep->ker", basis_in[:, 0], basis_in[:, 1], dens[:, 0], dens[:, 1]
    )
    coeffs = jnp.stack([coeff_re, coeff_im], 1).astype(jnp.bfloat16)
    everyone = lax.all_gather(coeffs.reshape(1, -1), "clus", axis=0, tiled=True)
    everyone = everyone.reshape(clusters, waves_dev, 2, exc, rank)
    stacked = jnp.transpose(everyone, (1, 2, 3, 0, 4)).reshape(waves_dev, 2, exc, clusters * rank)
    cluster_ids = lax.iota(jnp.int32, clusters)
    nearby = jnp.any(mine[:, None] == cluster_ids[None, :], axis=0)
    mask = far_mask(ranks[0], nearby, clusters, rank)
    couple = coupling[0]
    couple_re = jnp.where(mask, couple[:, 0], jnp.zeros_like(couple[:, 0]))
    couple_im = jnp.where(mask, couple[:, 1], jnp.zeros_like(couple[:, 1]))
    mixed_re, mixed_im = complex_product(
        "kim,kem->kei", couple_re, couple_im, stacked[:, 0], stacked[:, 1]
    )
    mixed_re = mixed_re.astype(jnp.bfloat16)
    mixed_im = mixed_im.astype(jnp.bfloat16)
    far_re, far_im = complex_product(
        "kip,kei->kep", basis_out[:, 0], basis_out[:, 1], mixed_re, mixed_im
    )
    return jnp.stack([near_re + far_re, near_im + far_im], 1).astype(jnp.bfloat16)


def solution(mesh):
    placed = (
        P("freq", None, "clus"),
        P("clus", None, "freq", None, None, None),
        P(),
        P("freq", None, None, "clus"),
        P("freq", None, None, "clus"),
        P("clus", "freq", None, None, None),
        P("clus", "freq", None),
    )
    return jax.shard_map(
        local, mesh=mesh, in_specs=placed, out_specs=P("freq", None, None, "clus"), check_vma=False
    )
```

profile of v0, /device:TPU:1, one launch (start us, length us, event | category | flops | bytes accessed | tf_op | source)
XLA Modules:
  0.0 167.0 jit_solution(12136194254410887922)
XLA Ops:
  6.5 2.4 %convolution_bitcast_fusion.1 = f32[512,1,8,128]{3,0,2,1:T(8,128)S(1)} fusion(s32[64]{0:T(128)S(1)} %iota_add_fusion, f32[64]{0:T(128)S(1)} %get-tuple-element.16, bf16[8,8,8,128]{3,2,1,0:T(8,128)(2,1)} %bitcast.167), kind=kOutput, calls=%fused_computation.9 | convolution fusion | flops 403144704 | bytes 2228736 | tf_op jit(solution)/shard_map/dot_general | solution.py:28
  9.0 2.4 %convolution_bitcast_fusion = f32[512,1,8,128]{3,0,2,1:T(8,128)S(1)} fusion(f32[64]{0:T(128)S(1)} %get-tuple-element.17, s32[64]{0:T(128)S(1)} %iota_add_fusion, bf16[8,8,8,128]{3,2,1,0:T(8,128)(2,1)} %bitcast.168), kind=kOutput, calls=%fused_computation.8 | convolution fusion | flops 403144704 | bytes 2228736 | tf_op jit(solution)/shard_map/dot_general | solution.py:29
  11.4 2.3 %pad_maximum_fusion = f32[512,2,8,128]{3,0,2,1:T(8,128)} fusion(f32[512,1,8,128]{3,0,2,1:T(8,128)S(1)} %convolution_bitcast_fusion, f32[512,1,8,128]{3,0,2,1:T(8,128)S(1)} %convolution_bitcast_fusion.1), kind=kLoop, calls=%fused_computation.3 | loop fusion | flops 1048576 | bytes 8388608 | tf_op jit(solution)/shard_map/stack | solution.py:30
  27.3 2.7 %and.71 = pred[32,32,16,32]{3,2,1,0:T(8,128)(4,1)S(1)} broadcast(pred[32,32,16]{2,1,0:T(8,128)(4,1)S(1)} %iota_compare_fusion), dimensions={0,1,2} | broadcast | bytes 540672 | tf_op jit(solution)/shard_map/and | solution.py:50
  30.1 3.6 %and.72 = pred[32,32,512]{2,1,0:T(32,128)(4,1)S(1)} reshape(pred[32,32,16,32]{3,2,1,0:T(8,128)(4,1)S(1)} %and.71) | data formatting | bytes 1048576 | tf_op jit(solution)/shard_map/and | solution.py:50
  33.7 10.5 %copy.129 = bf16[1,4,32,2,128,128]{5,4,1,2,3,0:T(8,128)(2,1)} copy(bf16[1,4,32,2,128,128]{5,4,3,2,1,0:T(8,128)(2,1)} %param.8) | data formatting | bytes 16777216 | tf_op args[1]
  44.2 54.4 %reduce-scatter.2.cloned.1.call-done = f32[32,2,8,128]{3,0,2,1:T(8,128)} async-done(((f32[512,2,8,128]{3,0,2,1:T(8,128)}), f32[32,2,8,128]{3,0,2,1:T(8,128)}) %reduce-scatter.2.cloned.1.call-update) | async-done | bytes 262160 | tf_op jit(solution)/shard_map/reduce_scatter | solution.py:61
  99.5 3.5 %collective-permute-start.5 = (bf16[32,2,8,128]{3,0,2,1:T(8,128)(2,1)S(1)}, bf16[32,2,8,128]{3,0,2,1:T(8,128)(2,1)S(1)}, u32[]{:S(2)}, u32[]{:S(2)}) collective-permute-start(bf16[32,2,8,128]{3,0,2,1:T(8,128)(2,1)S(1)} %convert_element_type.37), channel_id=1, source_target_pairs={{15,0},{0,1},{1,2},{2,3},{3,4},{4,5},{5,6},{6,7},{7,8},{8,9},{9,10... | collective-permute-start | bytes 393224 | tf_op jit(solution)/shard_map/ppermute | solution.py:14
  103.0 1.3 collective-permute-start.3
  104.3 1.4 collective-permute-start.2
  105.7 2.1 %collective-permute-start.1 = (bf16[32,2,8,128]{3,0,2,1:T(8,128)(2,1)S(1)}, bf16[32,2,8,128]{3,0,2,1:T(8,128)(2,1)}, u32[]{:S(2)}, u32[]{:S(2)}) collective-permute-start(bf16[32,2,8,128]{3,0,2,1:T(8,128)(2,1)S(1)} %convert_element_type.37), channel_id=1, source_target_pairs={{13,0},{14,1},{15,2},{0,3},{1,4},{2,5},{3,6},{4,7},{5,8},{6,9},{7,... | collective-permute-start | bytes 393224 | tf_op jit(solution)/shard_map/ppermute | solution.py:14
  109.0 21.1 %all-gather = bf16[16,1,16384]{2,1,0:T(2,128)(2,1)S(1)} all-gather(bf16[1,1,16384]{2,1,0:T(2,128)(2,1)S(1)} %reshape.79), channel_id=1, replica_groups=mesh['freq'=16,'clus'=16] {'clus'}, dimensions={0}, use_global_device_ids=true | all-gather | bytes 557056 | tf_op jit(solution)/shard_map/all_gather | solution.py:83
  130.1 3.1 %reduce = bf16[16,16384]{1,0:T(8,128)(2,1)S(1)} reduce(bf16[16,1,16384]{2,1,0:T(2,128)(2,1)S(1)} %all-gather, bf16[]{:T(256)} %constant.97), dimensions={1}, to_apply=%all-gather.reduce_sub_computation | reduce | bytes 1048578 | tf_op jit(solution)/shard_map/all_gather | solution.py:83
  133.3 1.6 reshape.77
  134.9 3.8 %copy.79 = bf16[32,2,8,16,32]{4,3,2,0,1:T(8,128)(2,1)} copy(bf16[32,2,8,16,32]{4,2,1,0,3:T(8,128)(2,1)S(1)} %bitcast.166) | data formatting | bytes 1048576 | tf_op jit(solution)/shard_map/transpose | solution.py:85
  138.7 3.5 %reshape.78 = bf16[32,2,8,512]{3,2,0,1:T(8,128)(2,1)S(1)} reshape(bf16[32,2,8,16,32]{4,3,2,0,1:T(8,128)(2,1)} %copy.79) | data formatting | bytes 1048576 | tf_op jit(solution)/shard_map/reshape | solution.py:85
  142.3 1.8 %fusion.22 = f32[32,8,32]{2,1,0:T(8,128)S(1)} fusion(pred[32,32,512]{2,1,0:T(32,128)(4,1)S(1)} %and.72, bf16[32,2,32,512]{3,2,1,0:T(8,128)(2,1)} %bitcast.170, pred[32,512]{1,0:T(8,128)(4,1)S(1)} %compare_and_fusion, bf16[32,2,8,512]{3,2,0,1:T(8,128)(2,1)S(1)} %reshape.78), kind=kOutput, calls=%fused_computation.40 | convolution fusion | flops 9437184 | bytes 1884160 | tf_op jit(solution)/shard_map/kim,kem->kei/dot_general | solution.py:38
  145.8 1.4 collective-permute-start
  147.3 4.8 %collective-permute-done = bf16[32,2,8,128]{3,0,2,1:T(8,128)(2,1)S(1)} collective-permute-done((bf16[32,2,8,128]{3,0,2,1:T(8,128)(2,1)S(1)}, bf16[32,2,8,128]{3,0,2,1:T(8,128)(2,1)S(1)}, u32[]{:S(2)}, u32[]{:S(2)}) %collective-permute-start) | collective-permute-done | bytes 131104 | tf_op jit(solution)/shard_map/ppermute | solution.py:14
  153.0 1.1 select_bitcast_fusion.2
  154.2 1.2 fusion.5
  155.4 1.2 fusion.4
  156.6 1.2 fusion.10
  157.8 1.2 fusion.11
  (64 shorter events, 8.3 us)
Async XLA Ops:
  6.5 92.0 %reduce-scatter.2.cloned.1.call-start = ((), (), s32[]{:S(2)}) async-start(), calls=%async_computation.1 | async-start | bytes 4456448 | tf_op jit(solution)/shard_map/reduce_scatter | solution.py:61
  13.7 0.7 copy-start.4
  13.7 13.2 %copy-start.3 = (s32[1,32,16]{1,2,0:T(8,128)S(1)}, s32[1,32,16]{1,2,0:T(8,128)}, u32[]{:S(2)}) copy-start(s32[1,32,16]{1,2,0:T(8,128)} %param.13) | copy-start | bytes 6148
  33.7 74.1 %copy-start = (bf16[32,2,32,128]{3,2,1,0:T(8,128)(2,1)S(1)}, bf16[32,2,32,128]{3,2,1,0:T(8,128)(2,1)}, u32[]{:S(2)}) copy-start(bf16[32,2,32,128]{3,2,1,0:T(8,128)(2,1)} %param.11) | copy-start | bytes 1572868
  99.5 46.3 %collective-permute-start.5 = (bf16[32,2,8,128]{3,0,2,1:T(8,128)(2,1)S(1)}, bf16[32,2,8,128]{3,0,2,1:T(8,128)(2,1)S(1)}, u32[]{:S(2)}, u32[]{:S(2)}) collective-permute-start(bf16[32,2,8,128]{3,0,2,1:T(8,128)(2,1)S(1)} %convert_element_type.37), channel_id=1, source_target_pairs={{15,0},{0,1},{1,2},{2,3},{3,4},{4,5},{5,6},{6,7},{7,8},{8,9},{9,10... | collective-permute-start | bytes 393224 | tf_op jit(solution)/shard_map/ppermute | solution.py:14
  103.0 44.2 %collective-permute-start.4 = (bf16[32,2,8,128]{3,0,2,1:T(8,128)(2,1)S(1)}, bf16[32,2,8,128]{3,0,2,1:T(8,128)(2,1)S(1)}, u32[]{:S(2)}, u32[]{:S(2)}) collective-permute-start(bf16[32,2,8,128]{3,0,2,1:T(8,128)(2,1)S(1)} %convert_element_type.37), channel_id=1, source_target_pairs={{1,0},{2,1},{3,2},{4,3},{5,4},{6,5},{7,6},{8,7},{9,8},{10,9},{11,1... | collective-permute-start | bytes 393224 | tf_op jit(solution)/shard_map/ppermute | solution.py:14
  103.0 44.2 %collective-permute-start.3 = (bf16[32,2,8,128]{3,0,2,1:T(8,128)(2,1)S(1)}, bf16[32,2,8,128]{3,0,2,1:T(8,128)(2,1)}, u32[]{:S(2)}, u32[]{:S(2)}) collective-permute-start(bf16[32,2,8,128]{3,0,2,1:T(8,128)(2,1)S(1)} %convert_element_type.37), channel_id=1, source_target_pairs={{14,0},{15,1},{0,2},{1,3},{2,4},{3,5},{4,6},{5,7},{6,8},{7,9},{8,1... | collective-permute-start | bytes 393224 | tf_op jit(solution)/shard_map/ppermute | solution.py:14
  104.3 43.0 %collective-permute-start.2 = (bf16[32,2,8,128]{3,0,2,1:T(8,128)(2,1)S(1)}, bf16[32,2,8,128]{3,0,2,1:T(8,128)(2,1)}, u32[]{:S(2)}, u32[]{:S(2)}) collective-permute-start(bf16[32,2,8,128]{3,0,2,1:T(8,128)(2,1)S(1)} %convert_element_type.37), channel_id=1, source_target_pairs={{2,0},{3,1},{4,2},{5,3},{6,4},{7,5},{8,6},{9,7},{10,8},{11,9},{12,... | collective-permute-start | bytes 393224 | tf_op jit(solution)/shard_map/ppermute | solution.py:14
  105.7 41.6 %collective-permute-start.1 = (bf16[32,2,8,128]{3,0,2,1:T(8,128)(2,1)S(1)}, bf16[32,2,8,128]{3,0,2,1:T(8,128)(2,1)}, u32[]{:S(2)}, u32[]{:S(2)}) collective-permute-start(bf16[32,2,8,128]{3,0,2,1:T(8,128)(2,1)S(1)} %convert_element_type.37), channel_id=1, source_target_pairs={{13,0},{14,1},{15,2},{0,3},{1,4},{2,5},{3,6},{4,7},{5,8},{6,9},{7,... | collective-permute-start | bytes 393224 | tf_op jit(solution)/shard_map/ppermute | solution.py:14
  138.7 5.3 %copy-start.5 = (bf16[1,32,2,32,512]{4,3,2,1,0:T(8,128)(2,1)S(1)}, bf16[1,32,2,32,512]{4,3,2,1,0:T(8,128)(2,1)}, u32[]{:S(2)}) copy-start(bf16[1,32,2,32,512]{4,3,2,1,0:T(8,128)(2,1)} %param.12) | copy-start | bytes 6291460
  142.2 2.2 %copy-start.6 = (bf16[1,32,2,32,512]{4,3,2,1,0:T(8,128)(2,1)S(1)}, bf16[1,32,2,32,512]{4,3,2,1,0:T(8,128)(2,1)}, u32[]{:S(2)}) copy-start(bf16[1,32,2,32,512]{4,3,2,1,0:T(8,128)(2,1)} %param.12) | copy-start | bytes 6291460
  142.2 12.0 %slice-start = ((s8[8388608]{0:T(1024)(128)(4,1)}), s8[4194304]{0:T(1024)(128)(4,1)S(1)}, s32[]{:S(2)}) async-start(s8[8388608]{0:T(1024)(128)(4,1)} %bitcast.160), calls=%async_computation.2 | async-start | bytes 8388608
  144.0 1.4 copy-start.1
  144.0 3.2 %copy-start.2 = (f32[32,2,8,128]{3,0,2,1:T(8,128)S(1)}, f32[32,2,8,128]{3,0,2,1:T(8,128)}, u32[]{:S(2)}) copy-start(f32[32,2,8,128]{3,0,2,1:T(8,128)} %reduce-scatter.2.cloned.1.call-done) | copy-start | bytes 786436
  144.4 9.8 %slice-start.1 = ((s8[8388608]{0:T(1024)(128)(4,1)}), s8[4194304]{0:T(1024)(128)(4,1)S(1)}, s32[]{:S(2)}) async-start(s8[8388608]{0:T(1024)(128)(4,1)} %bitcast.160), calls=%async_computation.3 | async-start | bytes 8388608
  145.8 6.2 %collective-permute-start = (bf16[32,2,8,128]{3,0,2,1:T(8,128)(2,1)S(1)}, bf16[32,2,8,128]{3,0,2,1:T(8,128)(2,1)S(1)}, u32[]{:S(2)}, u32[]{:S(2)}) collective-permute-start(bf16[32,2,8,128]{3,0,2,1:T(8,128)(2,1)S(1)} %convert_element_type.37), channel_id=1, source_target_pairs={{3,0},{4,1},{5,2},{6,3},{7,4},{8,5},{9,6},{10,7},{11,8},{12,9},{13... | collective-permute-start | bytes 393224 | tf_op jit(solution)/shard_map/ppermute | solution.py:14
Sparse Core Ops, SparseCore 0:
  13.8 84.7 reduce-scatter.1
where the time goes:
time: 167 us
  waiting for transfers between devices  59.2 us (35%)
  local copies, waits for them, and re-layouts  28.8 us (17%)
  between operations  25.1 us (15%)
  blocking collectives  21.1 us (13%)
  matrix products  14.3 us (9%)
  starting transfers between devices  9.65 us (6%)
  other arithmetic  8.77 us (5%)
    reduce_scatter x1, waiting for transfers between devices, local(): lax.psum_scatter(transform(history, cos_tab, sin_tab), 'freq', scatter_di...  54.4 us
    all_gather x1, blocking collectives, local(): everyone = lax.all_gather(coeffs.reshape(1, -1), 'clus', axis=0, tiled=True)  21.1 us
    unnamed x20, local copies, waits for them, and re-layouts  11.5 us
    ppermute x6, starting transfers between devices, from_behind(): return lax.ppermute(block, axis, route)  9.65 us
    dot_general x16, matrix products, product(): return jnp.einsum(form, left, right, preferred_element_type=jnp.float32)  9.46 us
    and x2, local copies, waits for them, and re-layouts, far_mask(): jnp.transpose(keep_out, (0, 2, 1))[:, :, :, None] & keep_in[:, None, :, :]  6.32 us
    ppermute x6, waiting for transfers between devices, from_behind(): return lax.ppermute(block, axis, route)  4.77 us
    transpose x1, local copies, waits for them, and re-layouts, local(): jnp.transpose(everyone, (1, 2, 3, 0, 4))  3.81 us
  transfers between devices with their start and end apart: 7, of which 2 were waited for; matrix products, arithmetic and copies ran while one was open for 21% of the time, Pallas kernels for 0%

commit v1 on v0

v1 whole, which is shorter than its diff:
```python
import math

import jax
import jax.numpy as jnp
from jax import lax
from jax.experimental import pallas as pl
from jax.experimental.pallas import tpu as pltpu
from jax.sharding import PartitionSpec as P

STEPS = 1024
F32 = jnp.float32
BF16 = jnp.bfloat16
VMEM = pltpu.VMEM
OFFSETS = (1, -1, 2, -2, 3, -3)


def params(mib=48):
    return pltpu.CompilerParams(vmem_limit_bytes=mib * 1024 * 1024)


def nt(a, b):
    return lax.dot_general(a, b, (((1,), (1,)), ((), ())), preferred_element_type=F32)


def nn(a, b):
    return lax.dot_general(a, b, (((1,), (0,)), ((), ())), preferred_element_type=F32)


def tn(a, b):
    return lax.dot_general(a, b, (((0,), (0,)), ((), ())), preferred_element_type=F32)


def from_behind(block, axis, distance):
    devices = range(lax.axis_size(axis))
    route = [((i - distance) % len(devices), i) for i in devices]
    return lax.ppermute(block, axis, route)


def pack_kernel(hist_ref, out_ref):
    exc = hist_ref.shape[1]
    slabs = jnp.swapaxes(hist_ref[...].astype(F32), 0, 1).astype(BF16)
    for copy in range(out_ref.shape[0] // exc):
        out_ref[copy * exc : (copy + 1) * exc] = slabs


def table_kernel(half_ref, hi_ref, lo_ref, base_c, base_s):
    dests, waves, lanes = 8, 32, 128
    count = dests * waves
    first = half_ref[0] * count
    wave = first + lax.broadcasted_iota(jnp.int32, (count, lanes), 0)
    step = lax.broadcasted_iota(jnp.int32, (count, lanes), 1)
    theta = lax.rem(wave * step, STEPS).astype(F32) * (2.0 * math.pi / STEPS)
    weight = jnp.exp(step.astype(F32) * (-math.log(2.0) / STEPS)) * STEPS ** (-0.5)
    base_c[...] = weight * jnp.cos(theta)
    base_s[...] = weight * jnp.sin(theta)
    sub = lax.broadcasted_iota(jnp.int32, (8, lanes), 0)
    for block in range(STEPS // lanes):
        gain = 2.0 ** (-block * lanes / STEPS)
        for part in range(2):
            phi = ((sub * block + 2 * part) & 7).astype(F32) * (math.pi / 4.0)
            turn_c = (gain * jnp.cos(phi))[None]
            turn_s = (gain * jnp.sin(phi))[None]
            for dest in range(dests):
                rows = slice(dest * waves, (dest + 1) * waves)
                tc = base_c[rows].reshape(waves // 8, 8, lanes)
                ts = base_s[rows].reshape(waves // 8, 8, lanes)
                value = (tc * turn_c - ts * turn_s).reshape(waves, lanes)
                hi = value.astype(BF16)
                lo = (value - hi.astype(F32)).astype(BF16)
                to = slice((dest * 2 + part) * waves, (dest * 2 + part + 1) * waves)
                hi_ref[to, block * lanes : (block + 1) * lanes] = hi
                lo_ref[to, block * lanes : (block + 1) * lanes] = lo


def transform_kernel(hi_ref, lo_ref, hist_ref, out_ref):
    hist = hist_ref[...].reshape(STEPS, 128)
    total = nn(hi_ref[...], hist) + nn(lo_ref[...], hist)
    out_ref[...] = total.astype(BF16).reshape(out_ref.shape)


def signs(shape):
    lane = lax.broadcasted_iota(jnp.int32, shape, len(shape) - 1)
    return jnp.where(lane < 64, -1.0, 1.0).astype(F32)


def coeff_kernel(recv_ref, basis_ref, dens_ref, coef_ref):
    waves = 32
    turned = jnp.swapaxes(recv_ref[...].astype(F32), 0, 1).reshape(2, waves, 8, 128)
    dens_ref[...] = jnp.swapaxes(turned, 0, 1).reshape(waves, 16, 128).astype(BF16)
    lane = lax.broadcasted_iota(jnp.int32, (32, 128), 1)
    lane_wave = (lane >> 3) & 7
    for group in range(waves // 8):
        right = turned[:, 8 * group : 8 * group + 8].reshape(128, 128).astype(BF16)
        left = basis_ref[8 * group : 8 * group + 8].reshape(512, 128)
        out = nt(left, right).reshape(8, 2, 32, 128)
        by_re = jnp.zeros((32, 128), F32)
        by_im = jnp.zeros((32, 128), F32)
        for wave in range(8):
            by_re = jnp.where(lane_wave == wave, out[wave, 0], by_re)
            by_im = jnp.where(lane_wave == wave, out[wave, 1], by_im)
        value = by_re + signs((32, 128)) * pltpu.roll(by_im, 64, 1)
        coef_ref[group * 32 : (group + 1) * 32] = value.astype(BF16)


def mask_kernel(mine_ref, ranks_ref, couple_ref, out_ref):
    waves, clusters, rank = ranks_ref.shape[0], ranks_ref.shape[1], couple_ref.shape[2]
    wide = clusters * rank
    ids = lax.broadcasted_iota(jnp.int32, (waves, clusters), 1)
    limit = ranks_ref[...]
    for slot in range(4):
        limit = jnp.where(ids == mine_ref[slot], 0, limit)
    row = lax.broadcasted_iota(jnp.int32, (clusters, wide), 0)
    col = lax.broadcasted_iota(jnp.int32, (clusters, wide), 1)
    spread = jnp.where((col >> 5) == row, 1.0, 0.0).astype(BF16)
    limits = nn(limit.astype(F32).astype(BF16), spread)
    inner = (lax.broadcasted_iota(jnp.int32, (waves, wide), 1) & 31).astype(F32)
    limits = jnp.where(inner < limits, limits, 0.0)
    outer = lax.broadcasted_iota(jnp.int32, (rank, wide), 0).astype(F32)
    for wave in range(waves):
        keep = outer < limits[wave : wave + 1]
        for part in range(2):
            block = couple_ref[wave, part].astype(F32)
            out_ref[wave, part] = jnp.where(keep, block, 0.0).astype(BF16)


def near_kernel(mine_ref, me_ref, blocks_ref, *refs):
    own_ref, moved_refs, out_ref = refs[0], refs[1:-1], refs[-1]
    waves = own_ref.shape[0]
    sources = [own_ref[...]]
    for slot in range(1, 4):
        offset = mine_ref[slot] - me_ref[0]
        picked = moved_refs[0][...]
        for moved, distance in zip(moved_refs[1:], OFFSETS[1:]):
            from_there = lax.rem(offset + distance + 32, 16) == 0
            picked = jnp.where(from_there, moved[...], picked)
        sources.append(picked)
    for wave in range(waves):
        total = nt(sources[0][wave], blocks_ref[0, wave].reshape(256, 128))
        for slot in range(1, 4):
            total += nt(sources[slot][wave], blocks_ref[slot, wave].reshape(256, 128))
        out_ref[wave, 0:8] = total[0:8, 0:128] - total[8:16, 128:256]
        out_ref[wave, 8:16] = total[8:16, 0:128] + total[0:8, 128:256]


def far_kernel(all_ref, couple_ref, basis_ref, near_ref, out_ref):
    row_wave = lax.broadcasted_iota(jnp.int32, (8, 32, 128), 0)
    lane_wave = (lax.broadcasted_iota(jnp.int32, (8, 32, 128), 2) >> 3) & 7
    same = row_wave == lane_wave
    sign = signs((256, 128))
    for group in range(4):
        waves = slice(8 * group, 8 * group + 8)
        right = all_ref[:, group * 32 : (group + 1) * 32].reshape(512, 128)
        left = couple_ref[waves].reshape(512, 512)
        out = nn(left, right).reshape(8, 2, 32, 128)
        by_re = out[:, 0].reshape(256, 128)
        by_im = out[:, 1].reshape(256, 128)
        mixed = by_re + sign * pltpu.roll(by_im, 64, 1)
        mixed = jnp.where(same.reshape(256, 128), mixed, 0.0).astype(BF16).astype(F32)
        turned = (sign * pltpu.roll(mixed, 64, 1)).astype(BF16)
        mixed = mixed.astype(BF16)
        basis_re = basis_ref[waves, 0].reshape(256, 128)
        basis_im = basis_ref[waves, 1].reshape(256, 128)
        far = tn(mixed, basis_re) + tn(turned, basis_im)
        far = jnp.swapaxes(far.reshape(2, 8, 8, 128), 0, 1).reshape(8, 16, 128)
        out_ref[waves] = (far + near_ref[waves]).astype(BF16)


def local(history, near_blocks, near_list, basis_out, basis_in, coupling, ranks):
    me = lax.axis_index("clus").astype(jnp.int32)
    mine = lax.dynamic_index_in_dim(near_list, me, 0, keepdims=False)
    half = (lax.axis_index("freq") // 8).astype(jnp.int32).reshape(1)
    smem = pl.BlockSpec(memory_space=pltpu.SMEM)
    vmem = pl.BlockSpec(memory_space=VMEM)
    groups = [list(range(8)), list(range(8, 16))]

    packed = pl.pallas_call(
        pack_kernel, out_shape=jax.ShapeDtypeStruct((16, 64, 128), BF16), compiler_params=params()
    )(history)
    mixed_in = lax.all_to_all(packed, "freq", 0, 0, tiled=True)
    hi, lo = pl.pallas_call(
        table_kernel,
        in_specs=[smem],
        out_shape=[jax.ShapeDtypeStruct((512, STEPS), BF16)] * 2,
        scratch_shapes=[VMEM((256, 128), F32)] * 2,
        compiler_params=params(),
    )(half)
    masked = pl.pallas_call(
        mask_kernel,
        in_specs=[smem, vmem, vmem],
        out_shape=jax.ShapeDtypeStruct((32, 2, 32, 512), BF16),
        compiler_params=params(),
    )(mine, ranks[0], coupling[0])
    spectrum = pl.pallas_call(
        transform_kernel, out_shape=jax.ShapeDtypeStruct((8, 64, 128), BF16), compiler_params=params()
    )(hi, lo, mixed_in)
    received = lax.all_to_all(spectrum, "freq", 0, 0, tiled=True, axis_index_groups=groups)
    dens, coeffs = pl.pallas_call(
        coeff_kernel,
        out_shape=[jax.ShapeDtypeStruct((32, 16, 128), BF16), jax.ShapeDtypeStruct((128, 128), BF16)],
        compiler_params=params(),
    )(received, basis_in)
    moved = [from_behind(dens, "clus", distance) for distance in OFFSETS]
    wide = jnp.broadcast_to(coeffs[None], (16, 128, 128))
    everyone = lax.all_to_all(wide, "clus", 0, 0, tiled=True)
    step = 4
    source = pl.BlockSpec((step, 16, 128), lambda i: (i, 0, 0))
    near = pl.pallas_call(
        near_kernel,
        grid=(32 // step,),
        in_specs=[smem, smem, pl.BlockSpec((4, step, 2, 128, 128), lambda i: (0, i, 0, 0, 0))] + [source] * 7,
        out_specs=pl.BlockSpec((step, 16, 128), lambda i: (i, 0, 0)),
        out_shape=jax.ShapeDtypeStruct((32, 16, 128), F32),
        compiler_params=params(),
    )(mine, me.reshape(1), near_blocks[0], dens, *moved)
    out = pl.pallas_call(
        far_kernel, out_shape=jax.ShapeDtypeStruct((32, 16, 128), BF16), compiler_params=params()
    )(everyone, masked, basis_out, near)
    return out.reshape(32, 2, 8, 128)


def solution(mesh):
    placed = (
        P("freq", None, "clus"),
        P("clus", None, "freq", None, None, None),
        P(),
        P("freq", None, None, "clus"),
        P("freq", None, None, "clus"),
        P("clus", "freq", None, None, None),
        P("clus", "freq", None),
    )
    return jax.shard_map(
        local, mesh=mesh, in_specs=placed, out_specs=P("freq", None, None, "clus"), check_vma=False
    )
```

time: 167 us -> 81.3 us (0.49)
  waiting for transfers between devices: 59.2 us -> 14.2 us
  between operations: 25.1 us -> 0.12 us
  starting transfers between devices: 9.65 us -> 30.2 us
  local copies, waits for them, and re-layouts: 28.8 us -> 13.8 us
  Pallas kernels: 0 us -> 14.5 us
  matrix products: 14.3 us -> 0 us
  blocking collectives: 21.1 us -> 7.89 us
  other arithmetic: 8.77 us -> 0 us
    reduce_scatter x1 -> x0, waiting for transfers between devices: 54.4 us -> none  [local(): lax.psum_scatter(transform(history, cos_tab, sin_tab), 'freq', scatter_di...]
    all_gather x1 -> x0, blocking collectives: 21.1 us -> none  [local(): everyone = lax.all_gather(coeffs.reshape(1, -1), 'clus', axis=0, tiled=True)]
    all_to_all x0 -> x2, starting transfers between devices: none -> 19.3 us  [the longest x1 11.7 us: local(): everyone = lax.all_to_all(wide, 'clus', 0, 0, tiled=True)]
    pallas_call x0 -> x7, Pallas kernels: none -> 14.5 us  [the longest x1 7.16 us: local(): pl.pallas_call(near_kernel, grid=(32 // step,), in_specs=[smem, smem, pl....]
    dot_general x18 -> x0, matrix products: 14.3 us -> none  [the longest x16 9.46 us: product(): return jnp.einsum(form, left, right, preferred_element_type=jnp.float32)]
    all_to_all x0 -> x1, blocking collectives: none -> 7.89 us  [local(): lax.all_to_all(spectrum, 'freq', 0, 0, tiled=True, axis_index_groups=groups)]
    and x4 -> x0, local copies, waits for them, and re-layouts: 6.48 us -> none  [the longest x2 6.32 us: far_mask(): jnp.transpose(keep_out, (0, 2, 1))[:, :, :, None] & keep_in[:, None, :, :]]
    all_to_all x0 -> x2, waiting for transfers between devices: none -> 6.02 us  [the longest x1 6.02 us: local(): mixed_in = lax.all_to_all(packed, 'freq', 0, 0, tiled=True)]
  transfers between devices with their start and end apart: 7 -> 8, of which waited for: 2 -> 2; matrix products, arithmetic and copies ran while one was open for 21% -> 1% of each run, Pallas kernels for 0% -> 12%
where the time goes in v1:
time: 81.3 us; the launch traced here: 80.7 us
  starting transfers between devices  30.2 us (37%)
  Pallas kernels  14.5 us (18%)
  waiting for transfers between devices  14.2 us (17%)
  local copies, waits for them, and re-layouts  13.8 us (17%)
  blocking collectives  7.89 us (10%)
    unnamed x39, local copies, waits for them, and re-layouts  12.7 us
    all_to_all x1, starting transfers between devices, local(): everyone = lax.all_to_all(wide, 'clus', 0, 0, tiled=True)  11.7 us
    ppermute x6, starting transfers between devices, from_behind(): return lax.ppermute(block, axis, route)  10.9 us
    ppermute x6, waiting for transfers between devices, from_behind(): return lax.ppermute(block, axis, route)  8.15 us
    all_to_all x1, blocking collectives, local(): lax.all_to_all(spectrum, 'freq', 0, 0, tiled=True, axis_index_groups=groups)  7.89 us
    all_to_all x1, starting transfers between devices, local(): mixed_in = lax.all_to_all(packed, 'freq', 0, 0, tiled=True)  7.58 us
    pallas_call x1, Pallas kernels, local(): pl.pallas_call(near_kernel, grid=(32 // step,), in_specs=[smem, smem, pl....  7.16 us
    all_to_all x1, waiting for transfers between devices, local(): mixed_in = lax.all_to_all(packed, 'freq', 0, 0, tiled=True)  6.02 us
  transfers between devices with their start and end apart: 8, of which 2 were waited for; matrix products, arithmetic and copies ran while one was open for 1% of the time, Pallas kernels for 12%

profile of v1, /device:TPU:1, one launch (start us, length us, event | category | flops | bytes accessed | tf_op | source)
XLA Modules:
  0.0 80.7 jit_solution(6566206972464924669)
XLA Ops:
  0.0 1.0 %copy-done.16 = bf16[64,8,128]{2,1,0:T(8,128)(2,1)S(1)} copy-done((bf16[64,8,128]{2,1,0:T(8,128)(2,1)S(1)}, bf16[64,8,128]{2,1,0:T(8,128)(2,1)}, u32[]{:S(2)}) %copy-start.16) | copy-done | bytes 131096
  1.0 0.8 shard_map.74
  1.8 7.6 %all-to-all-start = ((bf16[16,64,128]{2,1,0:T(8,128)(2,1)}), bf16[16,64,128]{2,1,0:T(8,128)(2,1)S(1)}, u32[]{:S(2)}, u32[]{:S(2)}) async-start(bf16[16,64,128]{2,1,0:T(8,128)(2,1)} %shard_map.74), calls=%async_computation | async-start | bytes 524288 | tf_op jit(solution)/shard_map/all_to_all | solution.py:179
  9.4 1.4 %shard_map.73 = (bf16[512,1024]{1,0:T(8,128)(2,1)S(1)}, bf16[512,1024]{1,0:T(8,128)(2,1)S(1)}) custom-call(s32[1]{0:T(128)} %bitcast.half_ref), custom_call_target="tpu_custom_call" | custom-call | tf_op jit(solution)/shard_map/pallas_call | solution.py:180
  10.8 6.0 %all-to-all-done.hist_ref = bf16[16,64,128]{2,1,0:T(8,128)(2,1)S(1)} async-done(((bf16[16,64,128]{2,1,0:T(8,128)(2,1)}), bf16[16,64,128]{2,1,0:T(8,128)(2,1)S(1)}, u32[]{:S(2)}, u32[]{:S(2)}) %all-to-all-start) | async-done | bytes 262176 | tf_op jit(solution)/shard_map/all_to_all | solution.py:179
  17.5 7.9 %all_to_all.15.recv_ref = bf16[8,64,128]{2,1,0:T(8,128)(2,1)S(1)} all-to-all(bf16[8,64,128]{2,1,0:T(8,128)(2,1)S(1)} %shard_map.75), channel_id=1, replica_groups={{0,16,32,48,64,80,96,112},{128,144,160,176,192,208,224,240},{1,17,33,49..., dimensions={0} | all-to-all | bytes 262144 | tf_op jit(solution)/shard_map/all_to_all | solution.py:196
  25.8 0.9 %broadcast_in_dim.2 = bf16[16,128,128]{2,1,0:T(8,128)(2,1)} broadcast(bf16[128,128]{1,0:T(8,128)(2,1)S(1)} %get-tuple-element.11), dimensions={1,2} | broadcast | bytes 557056 | tf_op jit(solution)/shard_map/broadcast_in_dim | solution.py:203
  26.7 11.7 %all-to-all-start.2 = ((bf16[16,128,128]{2,1,0:T(8,128)(2,1)}), bf16[16,128,128]{2,1,0:T(8,128)(2,1)S(1)}, u32[]{:S(2)}, u32[]{:S(2)}) async-start(bf16[16,128,128]{2,1,0:T(8,128)(2,1)} %broadcast_in_dim.2), calls=%async_computation.2 | async-start | bytes 1048576 | tf_op jit(solution)/shard_map/all_to_all | solution.py:204
  38.4 1.6 %collective-permute-start = (bf16[32,16,128]{2,1,0:T(8,128)(2,1)S(1)}, bf16[32,16,128]{2,1,0:T(8,128)(2,1)S(1)}, u32[]{:S(2)}, u32[]{:S(2)}) collective-permute-start(bf16[32,16,128]{2,1,0:T(8,128)(2,1)S(1)} %get-tuple-element.12.refs_0_), channel_id=1, source_target_pairs={{15,0},{0,1},{1,2},{2,3},{3,4},{4,5},{5,6},{6,7},{7,8},{8,9},{9,10... | collective-permute-start | bytes 393224 | tf_op jit(solution)/shard_map/ppermute | solution.py:36
  40.1 1.2 %collective-permute-start.2 = (bf16[32,16,128]{2,1,0:T(8,128)(2,1)S(1)}, bf16[32,16,128]{2,1,0:T(8,128)(2,1)S(1)}, u32[]{:S(2)}, u32[]{:S(2)}) collective-permute-start(bf16[32,16,128]{2,1,0:T(8,128)(2,1)S(1)} %get-tuple-element.12.refs_0_), channel_id=1, source_target_pairs={{14,0},{15,1},{0,2},{1,3},{2,4},{3,5},{4,6},{5,7},{6,8},{7,9},{8,1... | collective-permute-start | bytes 393224 | tf_op jit(solution)/shard_map/ppermute | solution.py:36
  41.3 1.5 %collective-permute-start.3 = (bf16[32,16,128]{2,1,0:T(8,128)(2,1)S(1)}, bf16[32,16,128]{2,1,0:T(8,128)(2,1)S(1)}, u32[]{:S(2)}, u32[]{:S(2)}) collective-permute-start(bf16[32,16,128]{2,1,0:T(8,128)(2,1)S(1)} %get-tuple-element.12.refs_0_), channel_id=1, source_target_pairs={{2,0},{3,1},{4,2},{5,3},{6,4},{7,5},{8,6},{9,7},{10,8},{11,9},{12,... | collective-permute-start | bytes 393224 | tf_op jit(solution)/shard_map/ppermute | solution.py:36
  42.7 2.0 %collective-permute-start.4 = (bf16[32,16,128]{2,1,0:T(8,128)(2,1)S(1)}, bf16[32,16,128]{2,1,0:T(8,128)(2,1)S(1)}, u32[]{:S(2)}, u32[]{:S(2)}) collective-permute-start(bf16[32,16,128]{2,1,0:T(8,128)(2,1)S(1)} %get-tuple-element.12.refs_0_), channel_id=1, source_target_pairs={{13,0},{14,1},{15,2},{0,3},{1,4},{2,5},{3,6},{4,7},{5,8},{6,9},{7,... | collective-permute-start | bytes 393224 | tf_op jit(solution)/shard_map/ppermute | solution.py:36
  44.7 8.1 %collective-permute-done.refs_1_ = bf16[32,16,128]{2,1,0:T(8,128)(2,1)S(1)} collective-permute-done((bf16[32,16,128]{2,1,0:T(8,128)(2,1)S(1)}, bf16[32,16,128]{2,1,0:T(8,128)(2,1)S(1)}, u32[]{:S(2)}, u32[]{:S(2)}) %collective-permute-start) | collective-permute-done | bytes 131104 | tf_op jit(solution)/shard_map/ppermute | solution.py:36
  52.9 4.6 %collective-permute-start.5 = (bf16[32,16,128]{2,1,0:T(8,128)(2,1)S(1)}, bf16[32,16,128]{2,1,0:T(8,128)(2,1)S(1)}, u32[]{:S(2)}, u32[]{:S(2)}) collective-permute-start(bf16[32,16,128]{2,1,0:T(8,128)(2,1)S(1)} %get-tuple-element.12.refs_0_), channel_id=1, source_target_pairs={{3,0},{4,1},{5,2},{6,3},{7,4},{8,5},{9,6},{10,7},{11,8},{12,9},{13... | collective-permute-start | bytes 393224 | tf_op jit(solution)/shard_map/ppermute | solution.py:36
  58.4 1.6 %copy-done.1 = bf16[1,32,2,32,512]{4,3,2,1,0:T(8,128)(2,1)S(1)} copy-done((bf16[1,32,2,32,512]{4,3,2,1,0:T(8,128)(2,1)S(1)}, bf16[1,32,2,32,512]{4,3,2,1,0:T(8,128)(2,1)}, u32[]{:S(2)}) %copy-start.1) | copy-done | bytes 2097176
  60.7 1.1 %shard_map.77.couple_ref = bf16[32,2,32,512]{3,2,1,0:T(8,128)(2,1)S(1)} custom-call(s32[4]{0:T(128)S(1)} %dynamic-slice_reduce_fusion.mine_ref, s32[32,16]{1,0:T(8,128)S(1)} %bitcast.7, bf16[32,2,32,512]{3,2,1,0:T(8,128)(2,1)S(1)} %bitcast.6), custom_call_target="tpu_custom_call" | custom-call | tf_op jit(solution)/shard_map/pallas_call | solution.py:187
  65.1 0.9 %copy-done.5 = bf16[32,16,128]{2,1,0:T(8,128)(2,1)S(1)} copy-done((bf16[32,16,128]{2,1,0:T(8,128)(2,1)S(1)}, bf16[32,16,128]{2,1,0:T(8,128)(2,1)}, u32[]{:S(2)}) %copy-start.5) | copy-done | bytes 131096
  66.0 0.9 %copy-done.7 = bf16[32,16,128]{2,1,0:T(8,128)(2,1)S(1)} copy-done((bf16[32,16,128]{2,1,0:T(8,128)(2,1)S(1)}, bf16[32,16,128]{2,1,0:T(8,128)(2,1)}, u32[]{:S(2)}) %copy-start.7) | copy-done | bytes 131096
  66.9 0.9 %copy-done.9 = bf16[32,16,128]{2,1,0:T(8,128)(2,1)S(1)} copy-done((bf16[32,16,128]{2,1,0:T(8,128)(2,1)S(1)}, bf16[32,16,128]{2,1,0:T(8,128)(2,1)}, u32[]{:S(2)}) %copy-start.9) | copy-done | bytes 131096
  67.8 0.9 %copy-done.11 = bf16[32,16,128]{2,1,0:T(8,128)(2,1)S(1)} copy-done((bf16[32,16,128]{2,1,0:T(8,128)(2,1)S(1)}, bf16[32,16,128]{2,1,0:T(8,128)(2,1)}, u32[]{:S(2)}) %copy-start.11) | copy-done | bytes 131096
  68.7 0.9 %copy-done.13 = bf16[32,16,128]{2,1,0:T(8,128)(2,1)S(1)} copy-done((bf16[32,16,128]{2,1,0:T(8,128)(2,1)S(1)}, bf16[32,16,128]{2,1,0:T(8,128)(2,1)}, u32[]{:S(2)}) %copy-start.13) | copy-done | bytes 131096
  69.6 0.9 %copy-done.15 = bf16[32,16,128]{2,1,0:T(8,128)(2,1)S(1)} copy-done((bf16[32,16,128]{2,1,0:T(8,128)(2,1)S(1)}, bf16[32,16,128]{2,1,0:T(8,128)(2,1)}, u32[]{:S(2)}) %copy-start.15) | copy-done | bytes 131096
  70.5 7.2 %shard_map.78.near_ref = f32[32,16,128]{2,1,0:T(8,128)S(1)} custom-call(s32[4]{0:T(128)S(1)} %dynamic-slice_reduce_fusion.mine_ref, s32[1]{0:T(128)} %bitcast.3.me_ref, bf16[4,32,2,128,128]{4,3,2,1,0:T(8,128)(2,1)} %bitcast.8, bf16[32,16,128]{2,1,0:T(8,128)(2,1)S(1)} %get-tuple-element.12.refs_0_, bf16[32,16,128]{2,1,0:T(8,128)(2,1)S(1)} %copy-done.5, ...), custom_call_target="tpu_custom_call" | custom-call | tf_op jit(solution)/shard_map/pallas_call | solution.py:207
  77.7 3.0 %shard_map.79 = bf16[32,16,128]{2,1,0:T(8,128)(2,1)} custom-call(bf16[16,128,128]{2,1,0:T(8,128)(2,1)S(1)} %all-to-all-done.2.all_ref, bf16[32,2,32,512]{3,2,1,0:T(8,128)(2,1)S(1)} %shard_map.77.couple_ref, bf16[32,2,32,128]{3,2,1,0:T(8,128)(2,1)S(1)} %copy-done.2, f32[32,16,128]{2,1,0:T(8,128)S(1)} %shard_map.78.near_ref), custom_call_target="tpu_custom_call" | custom-call | tf_op jit(solution)/shard_map/pallas_call | solution.py:215
  (41 shorter events, 6.0 us)
Async XLA Ops:
  0.0 58.2 %copy-start = (s32[16,4]{0,1:T(4,128)S(1)}, s32[16,4]{0,1:T(4,128)}, u32[]{:S(2)}) copy-start(s32[16,4]{0,1:T(4,128)} %param.9) | copy-start | bytes 772
  0.0 25.4 %copy-start.3 = (bf16[32,2,32,128]{3,2,1,0:T(8,128)(2,1)S(1)}, bf16[32,2,32,128]{3,2,1,0:T(8,128)(2,1)}, u32[]{:S(2)}) copy-start(bf16[32,2,32,128]{3,2,1,0:T(8,128)(2,1)} %basis_ref.2) | copy-start | bytes 1572868
  0.0 1.0 %copy-start.16 = (bf16[64,8,128]{2,1,0:T(8,128)(2,1)S(1)}, bf16[64,8,128]{2,1,0:T(8,128)(2,1)}, u32[]{:S(2)}) copy-start(bf16[64,8,128]{2,1,0:T(8,128)(2,1)} %hist_ref.1) | copy-start | bytes 393220
  1.8 15.0 %all-to-all-start = ((bf16[16,64,128]{2,1,0:T(8,128)(2,1)}), bf16[16,64,128]{2,1,0:T(8,128)(2,1)S(1)}, u32[]{:S(2)}, u32[]{:S(2)}) async-start(bf16[16,64,128]{2,1,0:T(8,128)(2,1)} %shard_map.74), calls=%async_computation | async-start | bytes 524288 | tf_op jit(solution)/shard_map/all_to_all | solution.py:179
  16.8 40.7 %copy-start.18 = (s32[1,32,16]{1,2,0:T(8,128)S(1)}, s32[1,32,16]{1,2,0:T(8,128)}, u32[]{:S(2)}) copy-start(s32[1,32,16]{1,2,0:T(8,128)} %param.13) | copy-start | bytes 6148
  26.7 51.0 %all-to-all-start.2 = ((bf16[16,128,128]{2,1,0:T(8,128)(2,1)}), bf16[16,128,128]{2,1,0:T(8,128)(2,1)S(1)}, u32[]{:S(2)}, u32[]{:S(2)}) async-start(bf16[16,128,128]{2,1,0:T(8,128)(2,1)} %broadcast_in_dim.2), calls=%async_computation.2 | async-start | bytes 1048576 | tf_op jit(solution)/shard_map/all_to_all | solution.py:204
  38.4 14.4 %collective-permute-start = (bf16[32,16,128]{2,1,0:T(8,128)(2,1)S(1)}, bf16[32,16,128]{2,1,0:T(8,128)(2,1)S(1)}, u32[]{:S(2)}, u32[]{:S(2)}) collective-permute-start(bf16[32,16,128]{2,1,0:T(8,128)(2,1)S(1)} %get-tuple-element.12.refs_0_), channel_id=1, source_target_pairs={{15,0},{0,1},{1,2},{2,3},{3,4},{4,5},{5,6},{6,7},{7,8},{8,9},{9,10... | collective-permute-start | bytes 393224 | tf_op jit(solution)/shard_map/ppermute | solution.py:36
  40.1 21.7 %collective-permute-start.1 = (bf16[32,16,128]{2,1,0:T(8,128)(2,1)S(1)}, bf16[32,16,128]{2,1,0:T(8,128)(2,1)S(1)}, u32[]{:S(2)}, u32[]{:S(2)}) collective-permute-start(bf16[32,16,128]{2,1,0:T(8,128)(2,1)S(1)} %get-tuple-element.12.refs_0_), channel_id=1, source_target_pairs={{1,0},{2,1},{3,2},{4,3},{5,4},{6,5},{7,6},{8,7},{9,8},{10,9},{11,1... | collective-permute-start | bytes 393224 | tf_op jit(solution)/shard_map/ppermute | solution.py:36
  40.1 22.4 %collective-permute-start.2 = (bf16[32,16,128]{2,1,0:T(8,128)(2,1)S(1)}, bf16[32,16,128]{2,1,0:T(8,128)(2,1)S(1)}, u32[]{:S(2)}, u32[]{:S(2)}) collective-permute-start(bf16[32,16,128]{2,1,0:T(8,128)(2,1)S(1)} %get-tuple-element.12.refs_0_), channel_id=1, source_target_pairs={{14,0},{15,1},{0,2},{1,3},{2,4},{3,5},{4,6},{5,7},{6,8},{7,9},{8,1... | collective-permute-start | bytes 393224 | tf_op jit(solution)/shard_map/ppermute | solution.py:36
  41.3 21.9 %collective-permute-start.3 = (bf16[32,16,128]{2,1,0:T(8,128)(2,1)S(1)}, bf16[32,16,128]{2,1,0:T(8,128)(2,1)S(1)}, u32[]{:S(2)}, u32[]{:S(2)}) collective-permute-start(bf16[32,16,128]{2,1,0:T(8,128)(2,1)S(1)} %get-tuple-element.12.refs_0_), channel_id=1, source_target_pairs={{2,0},{3,1},{4,2},{5,3},{6,4},{7,5},{8,6},{9,7},{10,8},{11,9},{12,... | collective-permute-start | bytes 393224 | tf_op jit(solution)/shard_map/ppermute | solution.py:36
  42.7 21.0 %collective-permute-start.4 = (bf16[32,16,128]{2,1,0:T(8,128)(2,1)S(1)}, bf16[32,16,128]{2,1,0:T(8,128)(2,1)S(1)}, u32[]{:S(2)}, u32[]{:S(2)}) collective-permute-start(bf16[32,16,128]{2,1,0:T(8,128)(2,1)S(1)} %get-tuple-element.12.refs_0_), channel_id=1, source_target_pairs={{13,0},{14,1},{15,2},{0,3},{1,4},{2,5},{3,6},{4,7},{5,8},{6,9},{7,... | collective-permute-start | bytes 393224 | tf_op jit(solution)/shard_map/ppermute | solution.py:36
  52.9 8.9 %copy-start.4 = (bf16[32,16,128]{2,1,0:T(8,128)(2,1)}, bf16[32,16,128]{2,1,0:T(8,128)(2,1)S(1)}, u32[]{:S(2)}) copy-start(bf16[32,16,128]{2,1,0:T(8,128)(2,1)S(1)} %collective-permute-done.refs_1_) | copy-start | bytes 393220
  52.9 11.6 %collective-permute-start.5 = (bf16[32,16,128]{2,1,0:T(8,128)(2,1)S(1)}, bf16[32,16,128]{2,1,0:T(8,128)(2,1)S(1)}, u32[]{:S(2)}, u32[]{:S(2)}) collective-permute-start(bf16[32,16,128]{2,1,0:T(8,128)(2,1)S(1)} %get-tuple-element.12.refs_0_), channel_id=1, source_target_pairs={{3,0},{4,1},{5,2},{6,3},{7,4},{8,5},{9,6},{10,7},{11,8},{12,9},{13... | collective-permute-start | bytes 393224 | tf_op jit(solution)/shard_map/ppermute | solution.py:36
  58.4 1.6 %copy-start.1 = (bf16[1,32,2,32,512]{4,3,2,1,0:T(8,128)(2,1)S(1)}, bf16[1,32,2,32,512]{4,3,2,1,0:T(8,128)(2,1)}, u32[]{:S(2)}) copy-start(bf16[1,32,2,32,512]{4,3,2,1,0:T(8,128)(2,1)} %param.12) | copy-start | bytes 6291460
  60.0 0.7 copy-start.17
  61.8 0.7 copy-start.6
  63.8 0.7 copy-start.12
  65.1 0.9 %copy-start.5 = (bf16[32,16,128]{2,1,0:T(8,128)(2,1)S(1)}, bf16[32,16,128]{2,1,0:T(8,128)(2,1)}, u32[]{:S(2)}) copy-start(bf16[32,16,128]{2,1,0:T(8,128)(2,1)} %copy-done.4) | copy-start | bytes 393220
  66.0 0.9 %copy-start.7 = (bf16[32,16,128]{2,1,0:T(8,128)(2,1)S(1)}, bf16[32,16,128]{2,1,0:T(8,128)(2,1)}, u32[]{:S(2)}) copy-start(bf16[32,16,128]{2,1,0:T(8,128)(2,1)} %copy-done.6) | copy-start | bytes 393220
  66.9 0.9 %copy-start.9 = (bf16[32,16,128]{2,1,0:T(8,128)(2,1)S(1)}, bf16[32,16,128]{2,1,0:T(8,128)(2,1)}, u32[]{:S(2)}) copy-start(bf16[32,16,128]{2,1,0:T(8,128)(2,1)} %copy-done.8) | copy-start | bytes 393220
  67.8 0.9 %copy-start.11 = (bf16[32,16,128]{2,1,0:T(8,128)(2,1)S(1)}, bf16[32,16,128]{2,1,0:T(8,128)(2,1)}, u32[]{:S(2)}) copy-start(bf16[32,16,128]{2,1,0:T(8,128)(2,1)} %copy-done.10) | copy-start | bytes 393220
  68.7 0.9 %copy-start.13 = (bf16[32,16,128]{2,1,0:T(8,128)(2,1)S(1)}, bf16[32,16,128]{2,1,0:T(8,128)(2,1)}, u32[]{:S(2)}) copy-start(bf16[32,16,128]{2,1,0:T(8,128)(2,1)} %copy-done.12) | copy-start | bytes 393220
  69.6 0.9 %copy-start.15 = (bf16[32,16,128]{2,1,0:T(8,128)(2,1)S(1)}, bf16[32,16,128]{2,1,0:T(8,128)(2,1)}, u32[]{:S(2)}) copy-start(bf16[32,16,128]{2,1,0:T(8,128)(2,1)} %copy-done.14) | copy-start | bytes 393220
  70.5 7.2 %copy-start.2 = (bf16[32,2,32,128]{3,2,1,0:T(8,128)(2,1)S(1)}, bf16[32,2,32,128]{3,2,1,0:T(8,128)(2,1)}, u32[]{:S(2)}) copy-start(bf16[32,2,32,128]{3,2,1,0:T(8,128)(2,1)} %basis_ref.3) | copy-start | bytes 1572868
  (3 other events, 1.9 us)

commit v2 on v1

v2 whole, which is shorter than its diff:
```python
import math

import jax
import jax.numpy as jnp
from jax import lax
from jax.experimental import pallas as pl
from jax.experimental.pallas import tpu as pltpu
from jax.sharding import PartitionSpec as P

STEPS = 1024
F32 = jnp.float32
BF16 = jnp.bfloat16
VMEM = pltpu.VMEM
FROM_EVEN = (1, -2, 2, -1, 3, -3)
FROM_ODD = (-1, -2, 2, -3, 1, 3)


def params(mib=12):
    return pltpu.CompilerParams(vmem_limit_bytes=mib * 1024 * 1024)


def nt(a, b):
    return lax.dot_general(a, b, (((1,), (1,)), ((), ())), preferred_element_type=F32)


def nn(a, b):
    return lax.dot_general(a, b, (((1,), (0,)), ((), ())), preferred_element_type=F32)


def tn(a, b):
    return lax.dot_general(a, b, (((0,), (0,)), ((), ())), preferred_element_type=F32)


def from_behind(block, axis, distance):
    devices = range(lax.axis_size(axis))
    route = [((i - distance) % len(devices), i) for i in devices]
    return lax.ppermute(block, axis, route)


def pack_kernel(hist_ref, out_ref):
    exc = hist_ref.shape[1]
    slabs = jnp.swapaxes(hist_ref[...].astype(F32), 0, 1).astype(BF16)
    for copy in range(out_ref.shape[0] // exc):
        out_ref[copy * exc : (copy + 1) * exc] = slabs


def fill_table(half, hi_ref, lo_ref, base_c, base_s):
    dests, waves, lanes = 8, 32, 128
    count = dests * waves
    first = half * count
    wave = first + lax.broadcasted_iota(jnp.int32, (count, lanes), 0)
    step = lax.broadcasted_iota(jnp.int32, (count, lanes), 1)
    theta = lax.rem(wave * step, STEPS).astype(F32) * (2.0 * math.pi / STEPS)
    weight = jnp.exp(step.astype(F32) * (-math.log(2.0) / STEPS)) * STEPS ** (-0.5)
    base_c[...] = weight * jnp.cos(theta)
    base_s[...] = weight * jnp.sin(theta)
    sub = lax.broadcasted_iota(jnp.int32, (8, lanes), 0)
    for block in range(STEPS // lanes):
        gain = 2.0 ** (-block * lanes / STEPS)
        for part in range(2):
            phi = ((sub * block + 2 * part) & 7).astype(F32) * (math.pi / 4.0)
            turn_c = (gain * jnp.cos(phi))[None]
            turn_s = (gain * jnp.sin(phi))[None]
            for dest in range(dests):
                rows = slice(dest * waves, (dest + 1) * waves)
                tc = base_c[rows].reshape(waves // 8, 8, lanes)
                ts = base_s[rows].reshape(waves // 8, 8, lanes)
                value = (tc * turn_c - ts * turn_s).reshape(waves, lanes)
                hi = value.astype(BF16)
                lo = (value - hi.astype(F32)).astype(BF16)
                to = slice((dest * 2 + part) * waves, (dest * 2 + part + 1) * waves)
                hi_ref[to, block * lanes : (block + 1) * lanes] = hi
                lo_ref[to, block * lanes : (block + 1) * lanes] = lo


def transform_kernel(hi_ref, lo_ref, hist_ref, out_ref):
    hist = hist_ref[...].reshape(STEPS, 128)
    total = nn(hi_ref[...], hist) + nn(lo_ref[...], hist)
    out_ref[...] = total.astype(BF16).reshape(out_ref.shape)


def signs(shape):
    lane = lax.broadcasted_iota(jnp.int32, shape, len(shape) - 1)
    return jnp.where(lane < 64, -1.0, 1.0).astype(F32)


def fill_masked(mine, ranks_ref, couple_ref, out_ref):
    clusters, waves = ranks_ref.shape
    rank, wide = couple_ref.shape[2], couple_ref.shape[3]
    ids = lax.broadcasted_iota(jnp.int32, (clusters, waves), 0)
    limit = ranks_ref[...]
    for shard in mine:
        limit = jnp.where(ids == shard, 0, limit)
    row = lax.broadcasted_iota(jnp.int32, (clusters, wide), 0)
    col = lax.broadcasted_iota(jnp.int32, (clusters, wide), 1)
    spread = jnp.where((col >> 5) == row, 1.0, 0.0).astype(BF16)
    limits = tn(limit.astype(F32).astype(BF16), spread)
    inner = (lax.broadcasted_iota(jnp.int32, (waves, wide), 1) & 31).astype(F32)
    limits = jnp.where(inner < limits, limits, 0.0)
    outer = lax.broadcasted_iota(jnp.int32, (rank, wide), 0).astype(F32)
    for wave in range(waves):
        keep = outer < limits[wave : wave + 1]
        for part in range(2):
            block = couple_ref[wave, part].astype(F32)
            out_ref[wave, part] = jnp.where(keep, block, 0.0).astype(BF16)


def table_kernel(info_ref, hi_ref, lo_ref, base_c, base_s):
    fill_table(info_ref[5], hi_ref, lo_ref, base_c, base_s)


def mask_kernel(info_ref, ranks_ref, couple_hbm, masked_ref, couple_ref, sem):
    copy = pltpu.make_async_copy(couple_hbm, couple_ref, sem)
    copy.start()
    copy.wait()
    fill_masked([info_ref[slot] for slot in range(4)], ranks_ref, couple_ref, masked_ref)


def turn_kernel(basis_ref, turned_ref):
    for group in range(4):
        for part in range(2):
            basis = basis_ref[8 * group : 8 * group + 8, part].reshape(256, 128)
            turned_ref[group, :, part * 256 : (part + 1) * 256] = basis.astype(F32).T.astype(BF16)


def fetch_kernel(from_hbm, to_ref, sem):
    copy = pltpu.make_async_copy(from_hbm, to_ref, sem)
    copy.start()
    copy.wait()


def coeff_kernel(recv_ref, basis_ref, masked_ref, turned_ref, dens_ref, coef_ref):
    waves = 32
    rows = jnp.swapaxes(recv_ref[...].astype(F32), 0, 1).reshape(2, waves, 8, 128)
    lane = lax.broadcasted_iota(jnp.int32, (32, 128), 1)
    lane_wave = (lane >> 3) & 7
    sign = signs((32, 128))
    for group in range(waves // 8):
        right = rows[:, 8 * group : 8 * group + 8].reshape(128, 128).T.astype(BF16)
        dens_ref[group] = right
        left = basis_ref[8 * group : 8 * group + 8].reshape(512, 128)
        out = nn(left, right).reshape(8, 2, 32, 128)
        by_re = jnp.zeros((32, 128), F32)
        by_im = jnp.zeros((32, 128), F32)
        for wave in range(8):
            by_re = jnp.where(lane_wave == wave, out[wave, 0], by_re)
            by_im = jnp.where(lane_wave == wave, out[wave, 1], by_im)
        value = (by_re + sign * pltpu.roll(by_im, 64, 1)).astype(BF16)
        for copy in range(coef_ref.shape[0]):
            coef_ref[copy, group * 32 : (group + 1) * 32] = value


def near_product(blocks, dens):
    lane = lax.broadcasted_iota(jnp.int32, (128, 128), 1)
    lane_wave = (lane >> 3) & 7
    dens = dens.astype(F32)
    left = [blocks[wave].reshape(256, 128) for wave in range(8)]
    right = [jnp.where(lane_wave == wave, dens, 0.0).astype(BF16) for wave in range(8)]
    return nn(jnp.concatenate(left, 1), jnp.concatenate(right, 0))


def block_copies(blocks_hbm, blocks_ref, sems, slots):
    return [
        [
            pltpu.make_async_copy(
                blocks_hbm.at[slot, pl.ds(8 * group, 8)], blocks_ref.at[at, group], sems.at[at, group]
            )
            for at, slot in enumerate(slots)
        ]
        for group in range(4)
    ]


def near_own_kernel(blocks_hbm, own_ref, out_ref, blocks_ref, sems):
    copies = block_copies(blocks_hbm, blocks_ref, sems, [0])
    for group in range(4):
        copies[group][0].start()
    for group in range(4):
        copies[group][0].wait()
        out_ref[group] = near_product(blocks_ref[0, group], own_ref[group])


def near_rest_kernel(info_ref, blocks_hbm, first_ref, *refs):
    moved_refs, (out_ref, blocks_ref, sems) = refs[:-3], refs[-3:]
    copies = block_copies(blocks_hbm, blocks_ref, sems, [1, 2, 3])
    for group in range(4):
        for copy in copies[group]:
            copy.start()
    me = info_ref[4]
    even = (me & 1) == 0
    sign = signs((128, 128))
    for group in range(4):
        total = first_ref[group]
        for slot in range(1, 4):
            offset = info_ref[slot] - me
            picked = moved_refs[0][group]
            for moved, for_even, for_odd in zip(moved_refs[1:], FROM_EVEN[1:], FROM_ODD[1:]):
                there = lax.rem(offset - jnp.where(even, for_even, for_odd) + 32, 16) == 0
                picked = jnp.where(there, moved[group], picked)
            copies[group][slot - 1].wait()
            total += near_product(blocks_ref[slot - 1, group], picked)
        out_ref[group] = total[:128] + sign * pltpu.roll(total[128:], 64, 1)


def far_kernel(info_ref, mine_ref, other_ref, couple_ref, turned_ref, near_ref, out_ref):
    even_core = (info_ref[4] & 1) == 0
    row_wave = lax.broadcasted_iota(jnp.int32, (8, 32, 128), 0)
    lane_wave = (lax.broadcasted_iota(jnp.int32, (8, 32, 128), 2) >> 3) & 7
    same = (row_wave == lane_wave).reshape(256, 128)
    sign = signs((256, 128))
    for group in range(4):
        waves = slice(8 * group, 8 * group + 8)
        mine = mine_ref[:, group * 32 : (group + 1) * 32]
        other = other_ref[:, group * 32 : (group + 1) * 32]
        evens = jnp.where(even_core, mine, other)
        odds = jnp.where(even_core, other, mine)
        right = jnp.stack([evens, odds], 1).reshape(512, 128)
        out = nn(couple_ref[waves].reshape(512, 512), right).reshape(8, 2, 32, 128)
        by_re = out[:, 0].reshape(256, 128)
        by_im = out[:, 1].reshape(256, 128)
        mixed = by_re + sign * pltpu.roll(by_im, 64, 1)
        mixed = jnp.where(same, mixed, 0.0).astype(BF16)
        swapped = (sign * pltpu.roll(mixed.astype(F32), 64, 1)).astype(BF16)
        total = nn(turned_ref[group], jnp.concatenate([mixed, swapped], 0)) + near_ref[group]
        total = jnp.swapaxes(total.T.reshape(2, 8, 8, 128), 0, 1)
        out_ref[waves] = total.reshape(8, 16, 128).astype(BF16)


def partner(block):
    size = lax.axis_size("clus")
    return lax.ppermute(block, "clus", [(i, i ^ 1) for i in range(size)])


def cross(block):
    size = lax.axis_size("clus")
    return lax.ppermute(block, "clus", [(i, (i + 1 if i % 2 else i - 1) % size) for i in range(size)])


def call(kernel, outs, specs=None, scratch=()):
    return pl.pallas_call(
        kernel,
        in_specs=specs,
        out_shape=outs,
        scratch_shapes=list(scratch),
        compiler_params=params(),
    )


def local(history, near_blocks, near_list, basis_out, basis_in, coupling, ranks):
    shape = jax.ShapeDtypeStruct
    me = lax.axis_index("clus").astype(jnp.int32)
    half = (lax.axis_index("freq") >> 3).astype(jnp.int32)
    mine = lax.dynamic_index_in_dim(near_list, me, 0, keepdims=False)
    info = jnp.concatenate([mine, me[None], half[None]])
    smem = pl.BlockSpec(memory_space=pltpu.SMEM)
    vmem = pl.BlockSpec(memory_space=VMEM)
    hbm = pl.BlockSpec(memory_space=pltpu.HBM)
    groups = [list(range(8)), list(range(8, 16))]
    cores = [[2 * z + core for z in range(8)] for core in range(2)]

    packed = call(pack_kernel, shape((16, 64, 128), BF16), [vmem])(history)
    steps = lax.all_to_all(packed, "freq", 0, 0, tiled=True)
    couple, outer, inner_hbm, blocks_hbm = [
        pltpu.with_memory_space_constraint(a, pltpu.HBM) for a in (coupling[0], basis_out, basis_in, near_blocks[0])
    ]
    dma = pltpu.SemaphoreType.DMA
    masked = call(
        mask_kernel, shape((32, 2, 32, 512), BF16), [smem, vmem, hbm], [VMEM((32, 2, 32, 512), BF16), dma]
    )(info, ranks[0].T, couple)
    turned = call(turn_kernel, shape((4, 128, 512), BF16), [vmem])(basis_out)
    hi, lo = call(
        table_kernel, [shape((512, STEPS), BF16)] * 2, [smem], [VMEM((256, 128), F32)] * 2
    )(info)
    inner = call(fetch_kernel, shape(inner_hbm.shape, BF16), [hbm], [dma])(inner_hbm)
    spectrum = call(transform_kernel, shape((8, 64, 128), BF16), [vmem] * 3)(hi, lo, steps)
    received = lax.all_to_all(spectrum, "freq", 0, 0, tiled=True, axis_index_groups=groups)
    dens, coeffs = call(
        coeff_kernel, [shape((4, 128, 128), BF16), shape((8, 128, 128), BF16)], [vmem] * 4
    )(received, inner, masked, turned)
    same_core = lax.all_to_all(coeffs, "clus", 0, 0, tiled=True, axis_index_groups=cores)
    beside = partner(dens)
    behind = from_behind(dens, "clus", 2)
    ahead = from_behind(dens, "clus", -2)
    first = call(
        near_own_kernel,
        shape((4, 256, 128), F32),
        [hbm, vmem],
        [VMEM((1, 4, 8, 2, 128, 128), BF16), pltpu.SemaphoreType.DMA((1, 4))],
    )(blocks_hbm, dens)
    beyond = cross(jnp.where((me & 1) == 1, behind, ahead))
    moved = [beside, behind, ahead, partner(behind), partner(ahead), beyond]
    near = call(
        near_rest_kernel,
        shape((4, 128, 128), F32),
        [smem, hbm] + [vmem] * 7,
        [VMEM((3, 4, 8, 2, 128, 128), BF16), pltpu.SemaphoreType.DMA((3, 4))],
    )(info, blocks_hbm, first, *moved)
    other_core = partner(same_core)
    out = call(far_kernel, shape((32, 16, 128), BF16), [smem] + [vmem] * 5)(
        info, same_core, other_core, masked, turned, near
    )
    return out.reshape(32, 2, 8, 128)


def solution(mesh):
    placed = (
        P("freq", None, "clus"),
        P("clus", None, "freq", None, None, None),
        P(),
        P("freq", None, None, "clus"),
        P("freq", None, None, "clus"),
        P("clus", "freq", None, None, None),
        P("clus", "freq", None),
    )
    return jax.shard_map(
        local, mesh=mesh, in_specs=placed, out_specs=P("freq", None, None, "clus"), check_vma=False
    )
```

time: 81.3 us -> 64.8 us (0.80)
  local copies, waits for them, and re-layouts: 13.8 us -> 1.16 us
  blocking collectives: 7.89 us -> 0 us
  Pallas kernels: 14.5 us -> 20.3 us
  waiting for transfers between devices: 14.2 us -> 11.2 us
  starting transfers between devices: 30.2 us -> 31.3 us
    unnamed x39 -> x8, local copies, waits for them, and re-layouts: 12.7 us -> 0.97 us
    ppermute x0 -> x5, starting transfers between devices: none -> 9.51 us  [the longest x4 9.34 us: partner(): return lax.ppermute(block, 'clus', [(i, i ^ 1) for i in range(size)])]
    ppermute x6 -> x2, starting transfers between devices: 10.9 us -> 2.7 us  [from_behind(): return lax.ppermute(block, axis, route)]
    ppermute x6 -> x2, waiting for transfers between devices: 8.15 us -> 0.01 us  [from_behind(): return lax.ppermute(block, axis, route)]
    all_to_all x1 -> x0, blocking collectives: 7.89 us -> none  [local(): lax.all_to_all(spectrum, 'freq', 0, 0, tiled=True, axis_index_groups=groups)]
    pallas_call x7 -> x10, Pallas kernels: 14.5 us -> 20.3 us  [the longest x1 5.5 us: local(): call(near_rest_kernel, shape((4, 128, 128), F32), [smem, hbm] + [vmem] *...]
    all_to_all x2 -> x3, waiting for transfers between devices: 6.02 us -> 9.39 us  [the longest x1 5.2 us: local(): steps = lax.all_to_all(packed, 'freq', 0, 0, tiled=True)]
    ppermute x0 -> x5, waiting for transfers between devices: none -> 1.85 us  [the longest x1 1.84 us: cross(): lax.ppermute(block, 'clus', [(i, (i + 1 if i % 2 else i - 1) % size) for...]
  transfers between devices with their start and end apart: 8 -> 10, of which waited for: 2 -> 4; matrix products, arithmetic and copies ran while one was open for 1% -> 0% of each run, Pallas kernels for 12% -> 21%
where the time goes in v2:
time: 64.8 us; the launch traced here: 64.3 us
  starting transfers between devices  31.3 us (48%)
  Pallas kernels  20.3 us (31%)
  waiting for transfers between devices  11.2 us (17%)
  local copies, waits for them, and re-layouts  1.16 us (2%)
    ppermute x4, starting transfers between devices, partner(): return lax.ppermute(block, 'clus', [(i, i ^ 1) for i in range(size)])  9.34 us
    all_to_all x1, starting transfers between devices, local(): lax.all_to_all(coeffs, 'clus', 0, 0, tiled=True, axis_index_groups=cores)  8.18 us
    all_to_all x1, starting transfers between devices, local(): steps = lax.all_to_all(packed, 'freq', 0, 0, tiled=True)  7.58 us
    pallas_call x1, Pallas kernels, local(): call(near_rest_kernel, shape((4, 128, 128), F32), [smem, hbm] + [vmem] *...  5.5 us
    all_to_all x1, waiting for transfers between devices, local(): steps = lax.all_to_all(packed, 'freq', 0, 0, tiled=True)  5.2 us
    pallas_call x1, Pallas kernels, local(): call(far_kernel, shape((32, 16, 128), BF16), [smem] + [vmem] * 5)  3.4 us
    all_to_all x1, starting transfers between devices, local(): lax.all_to_all(spectrum, 'freq', 0, 0, tiled=True, axis_index_groups=groups)  3.37 us
    all_to_all x1, waiting for transfers between devices, local(): lax.all_to_all(coeffs, 'clus', 0, 0, tiled=True, axis_index_groups=cores)  2.83 us
  transfers between devices with their start and end apart: 10, of which 4 were waited for; matrix products, arithmetic and copies ran while one was open for 0% of the time, Pallas kernels for 21%

profile of v2, /device:TPU:1, one launch (start us, length us, event | category | flops | bytes accessed | tf_op | source)
XLA Modules:
  0.0 64.3 jit_solution(10730664658617007796)
XLA Ops:
  0.0 1.0 %copy-done.2 = bf16[64,8,128]{2,1,0:T(8,128)(2,1)S(1)} copy-done((bf16[64,8,128]{2,1,0:T(8,128)(2,1)S(1)}, bf16[64,8,128]{2,1,0:T(8,128)(2,1)}, u32[]{:S(2)}) %copy-start.2) | copy-done | bytes 131096
  1.0 0.8 %shard_map.74 = bf16[16,64,128]{2,1,0:T(8,128)(2,1)} custom-call(bf16[64,8,128]{2,1,0:T(8,128)(2,1)S(1)} %copy-done.2), custom_call_target="tpu_custom_call" | custom-call | tf_op jit(solution)/shard_map/pallas_call | solution.py:261
  1.7 7.6 %all-to-all-start = ((bf16[16,64,128]{2,1,0:T(8,128)(2,1)}), bf16[16,64,128]{2,1,0:T(8,128)(2,1)S(1)}, u32[]{:S(2)}, u32[]{:S(2)}) async-start(bf16[16,64,128]{2,1,0:T(8,128)(2,1)} %shard_map.74), calls=%async_computation | async-start | bytes 524288 | tf_op jit(solution)/shard_map/all_to_all | solution.py:262
  9.3 0.2 dynamic-slice_reduce_fusion
  9.6 2.0 %shard_map.73 = (bf16[512,1024]{1,0:T(8,128)(2,1)S(1)}, bf16[512,1024]{1,0:T(8,128)(2,1)S(1)}) custom-call(s32[6]{0:T(128)S(1)} %pad_add_fusion.info_ref), custom_call_target="tpu_custom_call" | custom-call | tf_op jit(solution)/shard_map/pallas_call | solution.py:271
  11.6 5.2 %all-to-all-done.hist_ref = bf16[16,64,128]{2,1,0:T(8,128)(2,1)S(1)} async-done(((bf16[16,64,128]{2,1,0:T(8,128)(2,1)}), bf16[16,64,128]{2,1,0:T(8,128)(2,1)S(1)}, u32[]{:S(2)}, u32[]{:S(2)}) %all-to-all-start) | async-done | bytes 262176 | tf_op jit(solution)/shard_map/all_to_all | solution.py:262
  16.8 1.4 %shard_map.75 = bf16[8,64,128]{2,1,0:T(8,128)(2,1)} custom-call(bf16[512,1024]{1,0:T(8,128)(2,1)S(1)} %get-tuple-element.9.hi_ref, bf16[512,1024]{1,0:T(8,128)(2,1)S(1)} %get-tuple-element.10.lo_ref, bf16[16,64,128]{2,1,0:T(8,128)(2,1)S(1)} %all-to-all-done.hist_ref), custom_call_target="tpu_custom_call" | custom-call | tf_op jit(solution)/shard_map/pallas_call | solution.py:275
  18.2 3.4 %all-to-all-start.1 = ((bf16[8,64,128]{2,1,0:T(8,128)(2,1)}), bf16[8,64,128]{2,1,0:T(8,128)(2,1)S(1)}, u32[]{:S(2)}, u32[]{:S(2)}) async-start(bf16[8,64,128]{2,1,0:T(8,128)(2,1)} %shard_map.75), calls=%async_computation.1 | async-start | bytes 262144 | tf_op jit(solution)/shard_map/all_to_all | solution.py:276
  21.5 0.2 shard_map.78.turned_ref
  21.8 1.1 %shard_map.76.basis_ref = bf16[32,2,32,128]{3,2,1,0:T(8,128)(2,1)S(1)} custom-call(bf16[32,2,32,128]{3,2,1,0:T(8,128)(2,1)} %from_hbm.1), custom_call_target="tpu_custom_call" | custom-call | tf_op jit(solution)/shard_map/pallas_call | solution.py:274
  22.8 2.7 %shard_map.77.masked_ref.couple_ref = bf16[32,2,32,512]{3,2,1,0:T(8,128)(2,1)S(1)} custom-call(s32[6]{0:T(128)S(1)} %pad_add_fusion.info_ref, s32[16,32]{1,0:T(8,128)S(1)} %bitcast.8, bf16[32,2,32,512]{3,2,1,0:T(8,128)(2,1)} %bitcast.11), custom_call_target="tpu_custom_call" | custom-call | tf_op jit(solution)/shard_map/pallas_call | solution.py:267
  25.5 1.4 %all-to-all-done.1.recv_ref = bf16[8,64,128]{2,1,0:T(8,128)(2,1)S(1)} async-done(((bf16[8,64,128]{2,1,0:T(8,128)(2,1)}), bf16[8,64,128]{2,1,0:T(8,128)(2,1)S(1)}, u32[]{:S(2)}, u32[]{:S(2)}) %all-to-all-start.1) | async-done | bytes 131104 | tf_op jit(solution)/shard_map/all_to_all | solution.py:276
  26.9 1.2 %shard_map.79 = (bf16[4,128,128]{2,1,0:T(8,128)(2,1)S(1)}, bf16[8,128,128]{2,1,0:T(8,128)(2,1)}) custom-call(bf16[8,64,128]{2,1,0:T(8,128)(2,1)S(1)} %all-to-all-done.1.recv_ref, bf16[32,2,32,128]{3,2,1,0:T(8,128)(2,1)S(1)} %shard_map.76.basis_ref, bf16[32,2,32,512]{3,2,1,0:T(8,128)(2,1)S(1)} %shard_map.77.masked_ref.couple_ref, ...), custom_call_target="tpu_custom_call" | custom-call | tf_op jit(solution)/shard_map/pallas_call | solution.py:277
  28.1 8.2 %all-to-all-start.2 = ((bf16[8,128,128]{2,1,0:T(8,128)(2,1)}), bf16[8,128,128]{2,1,0:T(8,128)(2,1)S(1)}, u32[]{:S(2)}, u32[]{:S(2)}) async-start(bf16[8,128,128]{2,1,0:T(8,128)(2,1)} %get-tuple-element.11), calls=%async_computation.2 | async-start | bytes 524288 | tf_op jit(solution)/shard_map/all_to_all | solution.py:280
  36.2 1.5 %collective-permute-start.2 = (bf16[4,128,128]{2,1,0:T(8,128)(2,1)S(1)}, bf16[4,128,128]{2,1,0:T(8,128)(2,1)S(1)}, u32[]{:S(2)}, u32[]{:S(2)}) collective-permute-start(bf16[4,128,128]{2,1,0:T(8,128)(2,1)S(1)} %get-tuple-element.12.own_ref), channel_id=1, source_target_pairs={{14,0},{15,1},{0,2},{1,3},{2,4},{3,5},{4,6},{5,7},{6,8},{7,9},{8,1... | collective-permute-start | bytes 393224 | tf_op jit(solution)/shard_map/ppermute | solution.py:37
  37.7 1.2 %collective-permute-start.3 = (bf16[4,128,128]{2,1,0:T(8,128)(2,1)S(1)}, bf16[4,128,128]{2,1,0:T(8,128)(2,1)S(1)}, u32[]{:S(2)}, u32[]{:S(2)}) collective-permute-start(bf16[4,128,128]{2,1,0:T(8,128)(2,1)S(1)} %get-tuple-element.12.own_ref), channel_id=1, source_target_pairs={{2,0},{3,1},{4,2},{5,3},{6,4},{7,5},{8,6},{9,7},{10,8},{11,9},{12,... | collective-permute-start | bytes 393224 | tf_op jit(solution)/shard_map/ppermute | solution.py:37
  38.9 4.0 %collective-permute-start.1 = (bf16[4,128,128]{2,1,0:T(8,128)(2,1)S(1)}, bf16[4,128,128]{2,1,0:T(8,128)(2,1)S(1)}, u32[]{:S(2)}, u32[]{:S(2)}) collective-permute-start(bf16[4,128,128]{2,1,0:T(8,128)(2,1)S(1)} %get-tuple-element.12.own_ref), channel_id=1, source_target_pairs={{0,1},{1,0},{2,3},{3,2},{4,5},{5,4},{6,7},{7,6},{8,9},{9,8},{10,11... | collective-permute-start | bytes 393224 | tf_op jit(solution)/shard_map/ppermute | solution.py:231
  43.0 2.8 %all-to-all-done.2.mine_ref = bf16[8,128,128]{2,1,0:T(8,128)(2,1)S(1)} async-done(((bf16[8,128,128]{2,1,0:T(8,128)(2,1)}), bf16[8,128,128]{2,1,0:T(8,128)(2,1)S(1)}, u32[]{:S(2)}, u32[]{:S(2)}) %all-to-all-start.2) | async-done | bytes 262176 | tf_op jit(solution)/shard_map/all_to_all | solution.py:280
  45.8 4.8 %collective-permute-start = (bf16[8,128,128]{2,1,0:T(8,128)(2,1)S(1)}, bf16[8,128,128]{2,1,0:T(8,128)(2,1)S(1)}, u32[]{:S(2)}, u32[]{:S(2)}) collective-permute-start(bf16[8,128,128]{2,1,0:T(8,128)(2,1)S(1)} %all-to-all-done.2.mine_ref), channel_id=1, source_target_pairs={{0,1},{1,0},{2,3},{3,2},{4,5},{5,4},{6,7},{7,6},{8,9},{9,8},{10,11... | collective-permute-start | bytes 786440 | tf_op jit(solution)/shard_map/ppermute | solution.py:231
  50.9 0.5 collective-permute-start.5
  51.3 2.2 %shard_map.80.first_ref = f32[4,256,128]{2,1,0:T(8,128)S(1)} custom-call(bf16[4,32,2,128,128]{4,3,2,1,0:T(8,128)(2,1)} %bitcast.9, bf16[4,128,128]{2,1,0:T(8,128)(2,1)S(1)} %get-tuple-element.12.own_ref), custom_call_target="tpu_custom_call" | custom-call | tf_op jit(solution)/shard_map/pallas_call | solution.py:284
  53.5 1.8 %collective-permute-done.6.refs_5_ = bf16[4,128,128]{2,1,0:T(8,128)(2,1)S(1)} collective-permute-done((bf16[4,128,128]{2,1,0:T(8,128)(2,1)S(1)}, bf16[4,128,128]{2,1,0:T(8,128)(2,1)S(1)}, u32[]{:S(2)}, u32[]{:S(2)}) %collective-permute-start.6) | collective-permute-done | bytes 131104 | tf_op jit(solution)/shard_map/ppermute | solution.py:236
  55.4 5.5 %shard_map.81.near_ref = f32[4,128,128]{2,1,0:T(8,128)S(1)} custom-call(s32[6]{0:T(128)S(1)} %pad_add_fusion.info_ref, bf16[4,32,2,128,128]{4,3,2,1,0:T(8,128)(2,1)} %bitcast.10, f32[4,256,128]{2,1,0:T(8,128)S(1)} %shard_map.80.first_ref, bf16[4,128,128]{2,1,0:T(8,128)(2,1)S(1)} %collective-permute-done.1.refs_0_, ...), custom_call_target="tpu_custom_call" | custom-call | tf_op jit(solution)/shard_map/pallas_call | solution.py:292
  60.9 3.4 %shard_map.82 = bf16[32,16,128]{2,1,0:T(8,128)(2,1)} custom-call(s32[6]{0:T(128)S(1)} %pad_add_fusion.info_ref, bf16[8,128,128]{2,1,0:T(8,128)(2,1)S(1)} %all-to-all-done.2.mine_ref, bf16[8,128,128]{2,1,0:T(8,128)(2,1)S(1)} %collective-permute-done.other_ref, bf16[32,2,32,512]{3,2,1,0:T(8,128)(2,1)S(1)} %shard_map.77.masked_ref.couple_ref, ...), custom_call_target="tpu_custom_call" | custom-call | tf_op jit(solution)/shard_map/pallas_call | solution.py:299
  (17 shorter events, 0.4 us)
Async XLA Ops:
  0.0 9.3 %copy-start = (s32[16,4]{0,1:T(4,128)S(1)}, s32[16,4]{0,1:T(4,128)}, u32[]{:S(2)}) copy-start(s32[16,4]{0,1:T(4,128)} %param.9) | copy-start | bytes 772
  0.0 21.5 %copy-start.1 = (bf16[32,2,32,128]{3,2,1,0:T(8,128)(2,1)S(1)}, bf16[32,2,32,128]{3,2,1,0:T(8,128)(2,1)}, u32[]{:S(2)}) copy-start(bf16[32,2,32,128]{3,2,1,0:T(8,128)(2,1)} %basis_ref.1) | copy-start | bytes 1572868
  0.0 1.0 %copy-start.2 = (bf16[64,8,128]{2,1,0:T(8,128)(2,1)S(1)}, bf16[64,8,128]{2,1,0:T(8,128)(2,1)}, u32[]{:S(2)}) copy-start(bf16[64,8,128]{2,1,0:T(8,128)(2,1)} %hist_ref.1) | copy-start | bytes 393220
  1.7 15.0 %all-to-all-start = ((bf16[16,64,128]{2,1,0:T(8,128)(2,1)}), bf16[16,64,128]{2,1,0:T(8,128)(2,1)S(1)}, u32[]{:S(2)}, u32[]{:S(2)}) async-start(bf16[16,64,128]{2,1,0:T(8,128)(2,1)} %shard_map.74), calls=%async_computation | async-start | bytes 524288 | tf_op jit(solution)/shard_map/all_to_all | solution.py:262
  16.8 6.0 %copy-start.3 = (s32[1,32,16]{1,2,0:T(8,128)S(1)}, s32[1,32,16]{1,2,0:T(8,128)}, u32[]{:S(2)}) copy-start(s32[1,32,16]{1,2,0:T(8,128)} %param.13) | copy-start | bytes 6148
  18.2 8.7 %all-to-all-start.1 = ((bf16[8,64,128]{2,1,0:T(8,128)(2,1)}), bf16[8,64,128]{2,1,0:T(8,128)(2,1)S(1)}, u32[]{:S(2)}, u32[]{:S(2)}) async-start(bf16[8,64,128]{2,1,0:T(8,128)(2,1)} %shard_map.75), calls=%async_computation.1 | async-start | bytes 262144 | tf_op jit(solution)/shard_map/all_to_all | solution.py:276
  28.1 17.7 %all-to-all-start.2 = ((bf16[8,128,128]{2,1,0:T(8,128)(2,1)}), bf16[8,128,128]{2,1,0:T(8,128)(2,1)S(1)}, u32[]{:S(2)}, u32[]{:S(2)}) async-start(bf16[8,128,128]{2,1,0:T(8,128)(2,1)} %get-tuple-element.11), calls=%async_computation.2 | async-start | bytes 524288 | tf_op jit(solution)/shard_map/all_to_all | solution.py:280
  36.2 14.3 %collective-permute-start.2 = (bf16[4,128,128]{2,1,0:T(8,128)(2,1)S(1)}, bf16[4,128,128]{2,1,0:T(8,128)(2,1)S(1)}, u32[]{:S(2)}, u32[]{:S(2)}) collective-permute-start(bf16[4,128,128]{2,1,0:T(8,128)(2,1)S(1)} %get-tuple-element.12.own_ref), channel_id=1, source_target_pairs={{14,0},{15,1},{0,2},{1,3},{2,4},{3,5},{4,6},{5,7},{6,8},{7,9},{8,1... | collective-permute-start | bytes 393224 | tf_op jit(solution)/shard_map/ppermute | solution.py:37
  37.7 12.9 %collective-permute-start.3 = (bf16[4,128,128]{2,1,0:T(8,128)(2,1)S(1)}, bf16[4,128,128]{2,1,0:T(8,128)(2,1)S(1)}, u32[]{:S(2)}, u32[]{:S(2)}) collective-permute-start(bf16[4,128,128]{2,1,0:T(8,128)(2,1)S(1)} %get-tuple-element.12.own_ref), channel_id=1, source_target_pairs={{2,0},{3,1},{4,2},{5,3},{6,4},{7,5},{8,6},{9,7},{10,8},{11,9},{12,... | collective-permute-start | bytes 393224 | tf_op jit(solution)/shard_map/ppermute | solution.py:37
  38.9 14.6 %collective-permute-start.1 = (bf16[4,128,128]{2,1,0:T(8,128)(2,1)S(1)}, bf16[4,128,128]{2,1,0:T(8,128)(2,1)S(1)}, u32[]{:S(2)}, u32[]{:S(2)}) collective-permute-start(bf16[4,128,128]{2,1,0:T(8,128)(2,1)S(1)} %get-tuple-element.12.own_ref), channel_id=1, source_target_pairs={{0,1},{1,0},{2,3},{3,2},{4,5},{5,4},{6,7},{7,6},{8,9},{9,8},{10,11... | collective-permute-start | bytes 393224 | tf_op jit(solution)/shard_map/ppermute | solution.py:231
  45.8 15.1 %collective-permute-start = (bf16[8,128,128]{2,1,0:T(8,128)(2,1)S(1)}, bf16[8,128,128]{2,1,0:T(8,128)(2,1)S(1)}, u32[]{:S(2)}, u32[]{:S(2)}) collective-permute-start(bf16[8,128,128]{2,1,0:T(8,128)(2,1)S(1)} %all-to-all-done.2.mine_ref), channel_id=1, source_target_pairs={{0,1},{1,0},{2,3},{3,2},{4,5},{5,4},{6,7},{7,6},{8,9},{9,8},{10,11... | collective-permute-start | bytes 786440 | tf_op jit(solution)/shard_map/ppermute | solution.py:231
  50.6 4.8 %collective-permute-start.6 = (bf16[4,128,128]{2,1,0:T(8,128)(2,1)S(1)}, bf16[4,128,128]{2,1,0:T(8,128)(2,1)S(1)}, u32[]{:S(2)}, u32[]{:S(2)}) collective-permute-start(bf16[4,128,128]{2,1,0:T(8,128)(2,1)S(1)} %broadcast_select_fusion), channel_id=1, source_target_pairs={{0,15},{1,2},{2,1},{3,4},{4,3},{5,6},{6,5},{7,8},{8,7},{9,10},{10,... | collective-permute-start | bytes 393224 | tf_op jit(solution)/shard_map/ppermute | solution.py:236
  50.8 4.6 %collective-permute-start.4 = (bf16[4,128,128]{2,1,0:T(8,128)(2,1)S(1)}, bf16[4,128,128]{2,1,0:T(8,128)(2,1)S(1)}, u32[]{:S(2)}, u32[]{:S(2)}) collective-permute-start(bf16[4,128,128]{2,1,0:T(8,128)(2,1)S(1)} %collective-permute-done.2.refs_1_), channel_id=1, source_target_pairs={{0,1},{1,0},{2,3},{3,2},{4,5},{5,4},{6,7},{7,6},{8,9},{9,8},{10,11... | collective-permute-start | bytes 393224 | tf_op jit(solution)/shard_map/ppermute | solution.py:231
  50.9 4.5 %collective-permute-start.5 = (bf16[4,128,128]{2,1,0:T(8,128)(2,1)S(1)}, bf16[4,128,128]{2,1,0:T(8,128)(2,1)S(1)}, u32[]{:S(2)}, u32[]{:S(2)}) collective-permute-start(bf16[4,128,128]{2,1,0:T(8,128)(2,1)S(1)} %collective-permute-done.3.refs_2_), channel_id=1, source_target_pairs={{0,1},{1,0},{2,3},{3,2},{4,5},{5,4},{6,7},{7,6},{8,9},{9,8},{10,11... | collective-permute-start | bytes 393224 | tf_op jit(solution)/shard_map/ppermute | solution.py:231

commit v3 on v2

v3 whole, which is shorter than its diff:
```python
import math

import jax
import jax.numpy as jnp
from jax import lax
from jax.experimental import pallas as pl
from jax.experimental.pallas import tpu as pltpu
from jax.sharding import PartitionSpec as P

STEPS = 1024
F32 = jnp.float32
BF16 = jnp.bfloat16
VMEM = pltpu.VMEM
FROM_EVEN = (1, -2, 2, -1, 3, -3)
FROM_ODD = (-1, -2, 2, -3, 1, 3)


def params(mib=12):
    return pltpu.CompilerParams(vmem_limit_bytes=mib * 1024 * 1024)


def nt(a, b):
    return lax.dot_general(a, b, (((1,), (1,)), ((), ())), preferred_element_type=F32)


def nn(a, b):
    return lax.dot_general(a, b, (((1,), (0,)), ((), ())), preferred_element_type=F32)


def tn(a, b):
    return lax.dot_general(a, b, (((0,), (0,)), ((), ())), preferred_element_type=F32)


def from_behind(block, axis, distance):
    devices = range(lax.axis_size(axis))
    route = [((i - distance) % len(devices), i) for i in devices]
    return lax.ppermute(block, axis, route)


def pack_kernel(hist_ref, out_ref):
    exc = hist_ref.shape[1]
    slabs = jnp.swapaxes(hist_ref[...].astype(F32), 0, 1).astype(BF16)
    for copy in range(out_ref.shape[0] // exc):
        out_ref[copy * exc : (copy + 1) * exc] = slabs


def fill_table(half, hi_ref, lo_ref, base_c, base_s):
    dests, waves, lanes = 8, 32, 128
    count = dests * waves
    first = half * count
    wave = first + lax.broadcasted_iota(jnp.int32, (count, lanes), 0)
    step = lax.broadcasted_iota(jnp.int32, (count, lanes), 1)
    theta = lax.rem(wave * step, STEPS).astype(F32) * (2.0 * math.pi / STEPS)
    weight = jnp.exp(step.astype(F32) * (-math.log(2.0) / STEPS)) * STEPS ** (-0.5)
    base_c[...] = weight * jnp.cos(theta)
    base_s[...] = weight * jnp.sin(theta)
    sub = lax.broadcasted_iota(jnp.int32, (8, lanes), 0)
    for block in range(STEPS // lanes):
        gain = 2.0 ** (-block * lanes / STEPS)
        for part in range(2):
            phi = ((sub * block + 2 * part) & 7).astype(F32) * (math.pi / 4.0)
            turn_c = (gain * jnp.cos(phi))[None]
            turn_s = (gain * jnp.sin(phi))[None]
            for dest in range(dests):
                rows = slice(dest * waves, (dest + 1) * waves)
                tc = base_c[rows].reshape(waves // 8, 8, lanes)
                ts = base_s[rows].reshape(waves // 8, 8, lanes)
                value = (tc * turn_c - ts * turn_s).reshape(waves, lanes)
                hi = value.astype(BF16)
                lo = (value - hi.astype(F32)).astype(BF16)
                to = slice((dest * 2 + part) * waves, (dest * 2 + part + 1) * waves)
                hi_ref[to, block * lanes : (block + 1) * lanes] = hi
                lo_ref[to, block * lanes : (block + 1) * lanes] = lo


def transform_kernel(hi_ref, lo_ref, hist_ref, basis_ref, out_ref):
    hist = hist_ref[...].reshape(STEPS, 128)
    total = nn(hi_ref[...], hist) + nn(lo_ref[...], hist)
    out_ref[...] = total.astype(BF16).reshape(out_ref.shape)


def signs(shape):
    lane = lax.broadcasted_iota(jnp.int32, shape, len(shape) - 1)
    return jnp.where(lane < 64, -1.0, 1.0).astype(F32)


def mask_limits(mine, ranks_ref):
    clusters, waves = ranks_ref.shape
    rank, wide = 32, 512
    ids = lax.broadcasted_iota(jnp.int32, (clusters, waves), 0)
    limit = ranks_ref[...]
    for shard in mine:
        limit = jnp.where(ids == shard, 0, limit)
    row = lax.broadcasted_iota(jnp.int32, (clusters, wide), 0)
    col = lax.broadcasted_iota(jnp.int32, (clusters, wide), 1)
    spread = jnp.where((col >> 5) == row, 1.0, 0.0).astype(BF16)
    limits = tn(limit.astype(F32).astype(BF16), spread)
    inner = (lax.broadcasted_iota(jnp.int32, (waves, wide), 1) & 31).astype(F32)
    outer = lax.broadcasted_iota(jnp.int32, (rank, wide), 0).astype(F32)
    return jnp.where(inner < limits, limits, 0.0), outer


def table_kernel(info_ref, masked_hbm, hi_ref, lo_ref, base_c, base_s):
    fill_table(info_ref[5], hi_ref, lo_ref, base_c, base_s)


def mask_kernel(info_ref, ranks_ref, couple_hbm, masked_hbm, couple_ref, masked_ref, sems):
    copies = [
        pltpu.make_async_copy(couple_hbm.at[pl.ds(8 * group, 8)], couple_ref.at[group], sems.at[0, group])
        for group in range(4)
    ]
    for copy in copies:
        copy.start()
    limits, outer = mask_limits([info_ref[slot] for slot in range(4)], ranks_ref)
    back = []
    for group in range(4):
        copies[group].wait()
        for wave in range(8):
            at = 8 * group + wave
            keep = outer < limits[at : at + 1]
            for part in range(2):
                block = couple_ref[group, wave, part].astype(F32)
                masked_ref[group, wave, part] = jnp.where(keep, block, 0.0).astype(BF16)
        back.append(
            pltpu.make_async_copy(masked_ref.at[group], masked_hbm.at[pl.ds(8 * group, 8)], sems.at[1, group])
        )
        back[-1].start()
    for copy in back:
        copy.wait()


def dens_kernel(recv_ref, dens_ref):
    rows = jnp.swapaxes(recv_ref[...].astype(F32), 0, 1).reshape(2, 32, 8, 128)
    for group in range(4):
        dens_ref[group] = rows[:, 8 * group : 8 * group + 8].reshape(128, 128).T.astype(BF16)


def coeff_kernel(dens_ref, basis_ref, coef_ref):
    lane = lax.broadcasted_iota(jnp.int32, (32, 128), 1)
    lane_wave = (lane >> 3) & 7
    sign = signs((32, 128))
    products = [
        nn(basis_ref[8 * group : 8 * group + 8].reshape(512, 128), dens_ref[group]).reshape(8, 2, 32, 128)
        for group in range(4)
    ]
    for group, out in enumerate(products):
        by_re = jnp.zeros((32, 128), F32)
        by_im = jnp.zeros((32, 128), F32)
        for wave in range(8):
            by_re = jnp.where(lane_wave == wave, out[wave, 0], by_re)
            by_im = jnp.where(lane_wave == wave, out[wave, 1], by_im)
        value = (by_re + sign * pltpu.roll(by_im, 64, 1)).astype(BF16)
        for copy in range(coef_ref.shape[0]):
            coef_ref[copy, group * 32 : (group + 1) * 32] = value


def near_product(blocks, dens):
    lane = lax.broadcasted_iota(jnp.int32, (128, 128), 1)
    lane_wave = (lane >> 3) & 7
    dens = dens.astype(F32)
    left = [blocks[wave].reshape(256, 128) for wave in range(8)]
    right = [jnp.where(lane_wave == wave, dens, 0.0).astype(BF16) for wave in range(8)]
    return nn(jnp.concatenate(left, 1), jnp.concatenate(right, 0))


def near_own_kernel(blocks_hbm, own_ref, basis_ref, out_ref, rest_ref, turned_ref, blocks_ref, sems):
    copies = [
        pltpu.make_async_copy(blocks_hbm.at[0, pl.ds(8 * group, 8)], blocks_ref.at[group], sems.at[group])
        for group in range(4)
    ]
    rest = pltpu.make_async_copy(blocks_hbm.at[pl.ds(1, 3)], rest_ref, sems.at[4])
    for copy in copies:
        copy.start()
    rest.start()
    for group in range(4):
        for part in range(2):
            basis = basis_ref[8 * group : 8 * group + 8, part].reshape(256, 128)
            turned_ref[group, :, part * 256 : (part + 1) * 256] = basis.astype(F32).T.astype(BF16)
    for group in range(4):
        copies[group].wait()
        out_ref[group] = near_product(blocks_ref[group], own_ref[group])
    rest.wait()


def final_kernel(info_ref, blocks_ref, first_ref, mine_ref, other_ref, couple_ref, turned_ref, *refs):
    moved_refs, out_ref = refs[:-1], refs[-1]
    me = info_ref[4]
    even_core = (me & 1) == 0
    row_wave = lax.broadcasted_iota(jnp.int32, (8, 32, 128), 0)
    lane_wave = (lax.broadcasted_iota(jnp.int32, (8, 32, 128), 2) >> 3) & 7
    same = (row_wave == lane_wave).reshape(256, 128)
    sign = signs((256, 128))
    products = []
    for group in range(4):
        mine = mine_ref[:, group * 32 : (group + 1) * 32]
        other = other_ref[:, group * 32 : (group + 1) * 32]
        evens = jnp.where(even_core, mine, other)
        odds = jnp.where(even_core, other, mine)
        right = jnp.stack([evens, odds], 1).reshape(512, 128)
        left = couple_ref[8 * group : 8 * group + 8].reshape(512, 512)
        products.append(nn(left, right).reshape(8, 2, 32, 128))
    pairs = []
    for out in products:
        by_re = out[:, 0].reshape(256, 128)
        by_im = out[:, 1].reshape(256, 128)
        mixed = by_re + sign * pltpu.roll(by_im, 64, 1)
        mixed = jnp.where(same, mixed, 0.0).astype(BF16)
        swapped = (sign * pltpu.roll(mixed.astype(F32), 64, 1)).astype(BF16)
        pairs.append(jnp.concatenate([mixed, swapped], 0))
    fars = [nn(turned_ref[group], pairs[group]) for group in range(4)]
    for group in range(4):
        near = first_ref[group]
        for slot in range(1, 4):
            offset = info_ref[slot] - me
            picked = moved_refs[0][group]
            for moved, for_even, for_odd in zip(moved_refs[1:], FROM_EVEN[1:], FROM_ODD[1:]):
                there = lax.rem(offset - jnp.where(even_core, for_even, for_odd) + 32, 16) == 0
                picked = jnp.where(there, moved[group], picked)
            near += near_product(blocks_ref[slot - 1, 8 * group : 8 * group + 8], picked)
        total = near[:128] + sign[:128] * pltpu.roll(near[128:], 64, 1) + fars[group]
        total = jnp.swapaxes(total.T.reshape(2, 8, 8, 128), 0, 1)
        out_ref[8 * group : 8 * group + 8] = total.reshape(8, 16, 128).astype(BF16)


def partner(block):
    size = lax.axis_size("clus")
    return lax.ppermute(block, "clus", [(i, i ^ 1) for i in range(size)])


def cross(block):
    size = lax.axis_size("clus")
    return lax.ppermute(block, "clus", [(i, (i + 1 if i % 2 else i - 1) % size) for i in range(size)])


def call(kernel, outs, specs, scratch=(), out_specs=None):
    given = {} if out_specs is None else {"out_specs": out_specs}
    return pl.pallas_call(
        kernel,
        in_specs=specs,
        **given,
        out_shape=outs,
        scratch_shapes=list(scratch),
        compiler_params=params(),
    )


def local(history, near_blocks, near_list, basis_out, basis_in, coupling, ranks):
    shape = jax.ShapeDtypeStruct
    me = lax.axis_index("clus").astype(jnp.int32)
    half = (lax.axis_index("freq") >> 3).astype(jnp.int32)
    mine = lax.dynamic_index_in_dim(near_list, me, 0, keepdims=False)
    info = jnp.concatenate([mine, me[None], half[None]])
    smem = pl.BlockSpec(memory_space=pltpu.SMEM)
    vmem = pl.BlockSpec(memory_space=VMEM)
    hbm = pl.BlockSpec(memory_space=pltpu.HBM)
    groups = [list(range(8)), list(range(8, 16))]
    cores = [[2 * z + core for z in range(8)] for core in range(2)]

    packed = call(pack_kernel, shape((16, 64, 128), BF16), [vmem])(history)
    steps = lax.all_to_all(packed, "freq", 0, 0, tiled=True)
    couple, blocks_hbm = [pltpu.with_memory_space_constraint(a, pltpu.HBM) for a in (coupling[0], near_blocks[0])]
    dma = pltpu.SemaphoreType.DMA
    masked = call(
        mask_kernel,
        pltpu.HBM((32, 2, 32, 512), BF16),
        [smem, vmem, hbm],
        [VMEM((4, 8, 2, 32, 512), BF16), VMEM((4, 8, 2, 32, 512), BF16), dma((2, 4))],
        hbm,
    )(info, ranks[0].T, couple)
    hi, lo = call(
        table_kernel, [shape((512, STEPS), BF16)] * 2, [smem, hbm], [VMEM((256, 128), F32)] * 2
    )(info, pltpu.with_memory_space_constraint(masked, pltpu.HBM))
    spectrum = call(transform_kernel, shape((8, 64, 128), BF16), [vmem] * 4)(hi, lo, steps, basis_in)
    received = lax.all_to_all(spectrum, "freq", 0, 0, tiled=True, axis_index_groups=groups)
    dens = call(dens_kernel, shape((4, 128, 128), BF16), [vmem])(received)
    beside = partner(dens)
    behind = from_behind(dens, "clus", 2)
    ahead = from_behind(dens, "clus", -2)
    coeffs = call(coeff_kernel, shape((8, 128, 128), BF16), [vmem] * 2)(dens, basis_in)
    same_core = lax.all_to_all(coeffs, "clus", 0, 0, tiled=True, axis_index_groups=cores)
    beyond = cross(jnp.where((me & 1) == 1, behind, ahead))
    first, rest, turned = call(
        near_own_kernel,
        [shape((4, 256, 128), F32), shape((3, 32, 2, 128, 128), BF16), shape((4, 128, 512), BF16)],
        [hbm] + [vmem] * 2,
        [VMEM((4, 8, 2, 128, 128), BF16), dma((5,))],
    )(blocks_hbm, dens, basis_out)
    moved = [beside, behind, ahead, partner(behind), partner(ahead), beyond]
    other_core = partner(same_core)
    out = call(final_kernel, shape((32, 16, 128), BF16), [smem] + [vmem] * 12)(
        info, rest, first, same_core, other_core, masked, turned, *moved
    )
    return out.reshape(32, 2, 8, 128)


def solution(mesh):
    placed = (
        P("freq", None, "clus"),
        P("clus", None, "freq", None, None, None),
        P(),
        P("freq", None, None, "clus"),
        P("freq", None, None, "clus"),
        P("clus", "freq", None, None, None),
        P("clus", "freq", None),
    )
    return jax.shard_map(
        local, mesh=mesh, in_specs=placed, out_specs=P("freq", None, None, "clus"), check_vma=False
    )
```

time: 64.8 us -> 59.6 us (0.920)
  blocking collectives: 0 us -> 9.01 us
  waiting for transfers between devices: 11.2 us -> 4.48 us
  Pallas kernels: 20.3 us -> 15.3 us
  starting transfers between devices: 31.3 us -> 28.2 us
  local copies, waits for them, and re-layouts: 1.16 us -> 1.89 us
    all_to_all x0 -> x1, blocking collectives: none -> 9.01 us  [local(): lax.all_to_all(spectrum, 'freq', 0, 0, tiled=True, axis_index_groups=groups)]
    pallas_call x9 -> x7, Pallas kernels: 19.6 us -> 14.5 us  [the longest x1 4.09 us: local(): call(final_kernel, shape((32, 16, 128), BF16), [smem] + [vmem] * 12)]
    all_to_all x1, waiting for transfers between devices: 5.2 us -> 1.41 us  [local(): steps = lax.all_to_all(packed, 'freq', 0, 0, tiled=True)]
    all_to_all x1 -> x0, starting transfers between devices: 3.37 us -> none  [local(): lax.all_to_all(spectrum, 'freq', 0, 0, tiled=True, axis_index_groups=groups)]
    all_to_all x1, waiting for transfers between devices: 2.83 us -> 0.01 us  [local(): lax.all_to_all(coeffs, 'clus', 0, 0, tiled=True, axis_index_groups=cores)]
    ppermute x2, waiting for transfers between devices: 0.01 us -> 2.09 us  [from_behind(): return lax.ppermute(block, axis, route)]
    all_to_all x1 -> x0, waiting for transfers between devices: 1.36 us -> none  [local(): lax.all_to_all(spectrum, 'freq', 0, 0, tiled=True, axis_index_groups=groups)]
    ppermute x1, waiting for transfers between devices: 1.84 us -> 0.98 us  [cross(): lax.ppermute(block, 'clus', [(i, (i + 1 if i % 2 else i - 1) % size) for...]
  transfers between devices with their start and end apart: 10 -> 9, of which waited for: 4 -> 3; matrix products, arithmetic and copies ran while one was open for 0% -> 0% of each run, Pallas kernels for 21% -> 14%
where the time goes in v3:
time: 59.6 us; the launch traced here: 59.2 us
  starting transfers between devices  28.2 us (47%)
  Pallas kernels  15.3 us (26%)
  blocking collectives  9.01 us (15%)
  waiting for transfers between devices  4.48 us (8%)
  local copies, waits for them, and re-layouts  1.89 us (3%)
    ppermute x4, starting transfers between devices, partner(): return lax.ppermute(block, 'clus', [(i, i ^ 1) for i in range(size)])  9.52 us
    all_to_all x1, blocking collectives, local(): lax.all_to_all(spectrum, 'freq', 0, 0, tiled=True, axis_index_groups=groups)  9.01 us
    all_to_all x1, starting transfers between devices, local(): lax.all_to_all(coeffs, 'clus', 0, 0, tiled=True, axis_index_groups=cores)  8.19 us
    all_to_all x1, starting transfers between devices, local(): steps = lax.all_to_all(packed, 'freq', 0, 0, tiled=True)  7.58 us
    pallas_call x1, Pallas kernels, local(): call(final_kernel, shape((32, 16, 128), BF16), [smem] + [vmem] * 12)  4.09 us
    pallas_call x1, Pallas kernels, local(): call(near_own_kernel, [shape((4, 256, 128), F32), shape((3, 32, 2, 128, 1...  3.49 us
    pallas_call x1, Pallas kernels, local(): call(mask_kernel, pltpu.HBM((32, 2, 32, 512), BF16), [smem, vmem, hbm], [...  3.09 us
    ppermute x2, starting transfers between devices, from_behind(): return lax.ppermute(block, axis, route)  2.68 us
  transfers between devices with their start and end apart: 9, of which 3 were waited for; matrix products, arithmetic and copies ran while one was open for 0% of the time, Pallas kernels for 14%

profile of v3, /device:TPU:1, one launch (start us, length us, event | category | flops | bytes accessed | tf_op | source)
XLA Modules:
  0.0 59.2 jit_solution(13308083562813136857)
XLA Ops:
  0.0 1.0 %copy-done.4 = bf16[64,8,128]{2,1,0:T(8,128)(2,1)S(1)} copy-done((bf16[64,8,128]{2,1,0:T(8,128)(2,1)S(1)}, bf16[64,8,128]{2,1,0:T(8,128)(2,1)}, u32[]{:S(2)}) %copy-start.4) | copy-done | bytes 131096
  1.0 0.8 %shard_map.75 = bf16[16,64,128]{2,1,0:T(8,128)(2,1)} custom-call(bf16[64,8,128]{2,1,0:T(8,128)(2,1)S(1)} %copy-done.4), custom_call_target="tpu_custom_call" | custom-call | tf_op jit(solution)/shard_map/pallas_call | solution.py:259
  1.8 7.6 %all-to-all-start = ((bf16[16,64,128]{2,1,0:T(8,128)(2,1)}), bf16[16,64,128]{2,1,0:T(8,128)(2,1)S(1)}, u32[]{:S(2)}, u32[]{:S(2)}) async-start(bf16[16,64,128]{2,1,0:T(8,128)(2,1)} %shard_map.75), calls=%async_computation | async-start | bytes 524288 | tf_op jit(solution)/shard_map/all_to_all | solution.py:260
  9.4 0.2 dynamic-slice_reduce_fusion
  9.6 0.1 pad_add_fusion.info_ref
  9.7 0.7 %copy-done.5 = s32[1,32,16]{1,2,0:T(8,128)S(1)} copy-done((s32[1,32,16]{1,2,0:T(8,128)S(1)}, s32[1,32,16]{1,2,0:T(8,128)}, u32[]{:S(2)}) %copy-start.5) | copy-done | bytes 2072
  10.4 3.1 %shard_map.73.masked_hbm.couple_ref = bf16[32,2,32,512]{3,2,1,0:T(8,128)(2,1)} custom-call(s32[6]{0:T(128)S(1)} %pad_add_fusion.info_ref, s32[16,32]{1,0:T(8,128)S(1)} %bitcast.8, bf16[32,2,32,512]{3,2,1,0:T(8,128)(2,1)} %bitcast.10), custom_call_target="tpu_custom_call" | custom-call | tf_op jit(solution)/shard_map/pallas_call | solution.py:263
  13.5 2.0 %shard_map.74 = (bf16[512,1024]{1,0:T(8,128)(2,1)S(1)}, bf16[512,1024]{1,0:T(8,128)(2,1)S(1)}) custom-call(s32[6]{0:T(128)S(1)} %pad_add_fusion.info_ref, bf16[32,2,32,512]{3,2,1,0:T(8,128)(2,1)} %shard_map.73.masked_hbm.couple_ref), custom_call_target="tpu_custom_call" | custom-call | tf_op jit(solution)/shard_map/pallas_call | solution.py:270
  15.4 1.4 %all-to-all-done.hist_ref = bf16[16,64,128]{2,1,0:T(8,128)(2,1)S(1)} async-done(((bf16[16,64,128]{2,1,0:T(8,128)(2,1)}), bf16[16,64,128]{2,1,0:T(8,128)(2,1)S(1)}, u32[]{:S(2)}, u32[]{:S(2)}) %all-to-all-start) | async-done | bytes 262176 | tf_op jit(solution)/shard_map/all_to_all | solution.py:260
  16.8 0.7 %shard_map.76 = bf16[8,64,128]{2,1,0:T(8,128)(2,1)S(1)} custom-call(bf16[512,1024]{1,0:T(8,128)(2,1)S(1)} %get-tuple-element.10.hi_ref, bf16[512,1024]{1,0:T(8,128)(2,1)S(1)} %get-tuple-element.11.lo_ref, bf16[16,64,128]{2,1,0:T(8,128)(2,1)S(1)} %all-to-all-done.hist_ref, bf16[32,2,32,128]{3,2,1,0:T(8,128)(2,1)S(1)} %copy-done.2), custom_call_target="tpu_custom_call" | custom-call | tf_op jit(solution)/shard_map/pallas_call | solution.py:273
  17.6 9.0 %all_to_all.15.recv_ref = bf16[8,64,128]{2,1,0:T(8,128)(2,1)S(1)} all-to-all(bf16[8,64,128]{2,1,0:T(8,128)(2,1)S(1)} %shard_map.76), channel_id=1, replica_groups={{0,16,32,48,64,80,96,112},{128,144,160,176,192,208,224,240},{1,17,33,49..., dimensions={0} | all-to-all | bytes 262144 | tf_op jit(solution)/shard_map/all_to_all | solution.py:274
  26.6 0.1 shard_map.77.own_ref.dens_ref
  26.7 1.1 %shard_map.79 = bf16[8,128,128]{2,1,0:T(8,128)(2,1)} custom-call(bf16[4,128,128]{2,1,0:T(8,128)(2,1)S(1)} %shard_map.77.own_ref.dens_ref, bf16[32,2,32,128]{3,2,1,0:T(8,128)(2,1)S(1)} %copy-done.2), custom_call_target="tpu_custom_call" | custom-call | tf_op jit(solution)/shard_map/pallas_call | solution.py:279
  27.8 8.2 %all-to-all-start.2 = ((bf16[8,128,128]{2,1,0:T(8,128)(2,1)}), bf16[8,128,128]{2,1,0:T(8,128)(2,1)S(1)}, u32[]{:S(2)}, u32[]{:S(2)}) async-start(bf16[8,128,128]{2,1,0:T(8,128)(2,1)} %shard_map.79), calls=%async_computation.2 | async-start | bytes 524288 | tf_op jit(solution)/shard_map/all_to_all | solution.py:280
  36.0 2.7 %collective-permute-start.3 = (bf16[4,128,128]{2,1,0:T(8,128)(2,1)S(1)}, bf16[4,128,128]{2,1,0:T(8,128)(2,1)S(1)}, u32[]{:S(2)}, u32[]{:S(2)}) collective-permute-start(bf16[4,128,128]{2,1,0:T(8,128)(2,1)S(1)} %shard_map.77.own_ref.dens_ref), channel_id=1, source_target_pairs={{2,0},{3,1},{4,2},{5,3},{6,4},{7,5},{8,6},{9,7},{10,8},{11,9},{12,... | collective-permute-start | bytes 393224 | tf_op jit(solution)/shard_map/ppermute | solution.py:37
  38.6 0.0 collective-permute-start.2
  38.7 3.5 %collective-permute-start.1 = (bf16[4,128,128]{2,1,0:T(8,128)(2,1)S(1)}, bf16[4,128,128]{2,1,0:T(8,128)(2,1)S(1)}, u32[]{:S(2)}, u32[]{:S(2)}) collective-permute-start(bf16[4,128,128]{2,1,0:T(8,128)(2,1)S(1)} %shard_map.77.own_ref.dens_ref), channel_id=1, source_target_pairs={{0,1},{1,0},{2,3},{3,2},{4,5},{5,4},{6,7},{7,6},{8,9},{9,8},{10,11... | collective-permute-start | bytes 393224 | tf_op jit(solution)/shard_map/ppermute | solution.py:227
  42.2 2.1 %collective-permute-done.3.refs_2_ = bf16[4,128,128]{2,1,0:T(8,128)(2,1)S(1)} collective-permute-done((bf16[4,128,128]{2,1,0:T(8,128)(2,1)S(1)}, bf16[4,128,128]{2,1,0:T(8,128)(2,1)S(1)}, u32[]{:S(2)}, u32[]{:S(2)}) %collective-permute-start.3) | collective-permute-done | bytes 131104 | tf_op jit(solution)/shard_map/ppermute | solution.py:37
  44.2 3.5 %collective-permute-start.5 = (bf16[4,128,128]{2,1,0:T(8,128)(2,1)S(1)}, bf16[4,128,128]{2,1,0:T(8,128)(2,1)S(1)}, u32[]{:S(2)}, u32[]{:S(2)}) collective-permute-start(bf16[4,128,128]{2,1,0:T(8,128)(2,1)S(1)} %collective-permute-done.3.refs_2_), channel_id=1, source_target_pairs={{0,1},{1,0},{2,3},{3,2},{4,5},{5,4},{6,7},{7,6},{8,9},{9,8},{10,11... | collective-permute-start | bytes 393224 | tf_op jit(solution)/shard_map/ppermute | solution.py:227
  47.7 2.5 %collective-permute-start = (bf16[8,128,128]{2,1,0:T(8,128)(2,1)S(1)}, bf16[8,128,128]{2,1,0:T(8,128)(2,1)S(1)}, u32[]{:S(2)}, u32[]{:S(2)}) collective-permute-start(bf16[8,128,128]{2,1,0:T(8,128)(2,1)S(1)} %all-to-all-done.2.mine_ref), channel_id=1, source_target_pairs={{0,1},{1,0},{2,3},{3,2},{4,5},{5,4},{6,7},{7,6},{8,9},{9,8},{10,11... | collective-permute-start | bytes 786440 | tf_op jit(solution)/shard_map/ppermute | solution.py:227
  50.3 0.3 collective-permute-start.6
  50.6 3.5 %shard_map.78 = (f32[4,256,128]{2,1,0:T(8,128)S(1)}, bf16[3,32,2,128,128]{4,3,2,1,0:T(8,128)(2,1)S(1)}, bf16[4,128,512]{2,1,0:T(8,128)(2,1)S(1)}) custom-call(bf16[4,32,2,128,128]{4,3,2,1,0:T(8,128)(2,1)} %bitcast.9, bf16[4,128,128]{2,1,0:T(8,128)(2,1)S(1)} %shard_map.77.own_ref.dens_ref, bf16[32,2,32,128]{3,2,1,0:T(8,128)(2,1)S(1)} %copy-done.3), custom_call_target="tpu_custom_call" | custom-call | tf_op jit(solution)/shard_map/pallas_call | solution.py:282
  54.1 1.0 %collective-permute-done.6.refs_5_ = bf16[4,128,128]{2,1,0:T(8,128)(2,1)S(1)} collective-permute-done((bf16[4,128,128]{2,1,0:T(8,128)(2,1)S(1)}, bf16[4,128,128]{2,1,0:T(8,128)(2,1)S(1)}, u32[]{:S(2)}, u32[]{:S(2)}) %collective-permute-start.6) | collective-permute-done | bytes 131104 | tf_op jit(solution)/shard_map/ppermute | solution.py:232
  55.1 4.1 %shard_map.80 = bf16[32,16,128]{2,1,0:T(8,128)(2,1)} custom-call(s32[6]{0:T(128)S(1)} %pad_add_fusion.info_ref, bf16[3,32,2,128,128]{4,3,2,1,0:T(8,128)(2,1)S(1)} %get-tuple-element.12.blocks_ref, f32[4,256,128]{2,1,0:T(8,128)S(1)} %get-tuple-element.13.first_ref, bf16[8,128,128]{2,1,0:T(8,128)(2,1)S(1)} %all-to-all-done.2.mine_ref, ...), custom_call_target="tpu_custom_call" | custom-call | tf_op jit(solution)/shard_map/pallas_call | solution.py:290
  (18 shorter events, 0.1 us)
Async XLA Ops:
  0.0 9.4 %copy-start = (s32[16,4]{0,1:T(4,128)S(1)}, s32[16,4]{0,1:T(4,128)}, u32[]{:S(2)}) copy-start(s32[16,4]{0,1:T(4,128)} %param.9) | copy-start | bytes 772
  0.0 16.8 %copy-start.2 = (bf16[32,2,32,128]{3,2,1,0:T(8,128)(2,1)S(1)}, bf16[32,2,32,128]{3,2,1,0:T(8,128)(2,1)}, u32[]{:S(2)}) copy-start(bf16[32,2,32,128]{3,2,1,0:T(8,128)(2,1)} %basis_ref.5) | copy-start | bytes 1572868
  0.0 50.6 %copy-start.3 = (bf16[32,2,32,128]{3,2,1,0:T(8,128)(2,1)S(1)}, bf16[32,2,32,128]{3,2,1,0:T(8,128)(2,1)}, u32[]{:S(2)}) copy-start(bf16[32,2,32,128]{3,2,1,0:T(8,128)(2,1)} %basis_ref.4) | copy-start | bytes 1572868
  0.0 1.0 %copy-start.4 = (bf16[64,8,128]{2,1,0:T(8,128)(2,1)S(1)}, bf16[64,8,128]{2,1,0:T(8,128)(2,1)}, u32[]{:S(2)}) copy-start(bf16[64,8,128]{2,1,0:T(8,128)(2,1)} %hist_ref.1) | copy-start | bytes 393220
  1.8 15.0 %all-to-all-start = ((bf16[16,64,128]{2,1,0:T(8,128)(2,1)}), bf16[16,64,128]{2,1,0:T(8,128)(2,1)S(1)}, u32[]{:S(2)}, u32[]{:S(2)}) async-start(bf16[16,64,128]{2,1,0:T(8,128)(2,1)} %shard_map.75), calls=%async_computation | async-start | bytes 524288 | tf_op jit(solution)/shard_map/all_to_all | solution.py:260
  9.7 0.7 %copy-start.5 = (s32[1,32,16]{1,2,0:T(8,128)S(1)}, s32[1,32,16]{1,2,0:T(8,128)}, u32[]{:S(2)}) copy-start(s32[1,32,16]{1,2,0:T(8,128)} %param.13) | copy-start | bytes 6148
  17.6 37.5 %copy-start.1 = (bf16[32,2,32,512]{3,2,1,0:T(8,128)(2,1)S(1)}, bf16[32,2,32,512]{3,2,1,0:T(8,128)(2,1)}, u32[]{:S(2)}) copy-start(bf16[32,2,32,512]{3,2,1,0:T(8,128)(2,1)} %shard_map.73.masked_hbm.couple_ref) | copy-start | bytes 6291460
  27.8 19.9 %all-to-all-start.2 = ((bf16[8,128,128]{2,1,0:T(8,128)(2,1)}), bf16[8,128,128]{2,1,0:T(8,128)(2,1)S(1)}, u32[]{:S(2)}, u32[]{:S(2)}) async-start(bf16[8,128,128]{2,1,0:T(8,128)(2,1)} %shard_map.79), calls=%async_computation.2 | async-start | bytes 524288 | tf_op jit(solution)/shard_map/all_to_all | solution.py:280
  36.0 8.3 %collective-permute-start.3 = (bf16[4,128,128]{2,1,0:T(8,128)(2,1)S(1)}, bf16[4,128,128]{2,1,0:T(8,128)(2,1)S(1)}, u32[]{:S(2)}, u32[]{:S(2)}) collective-permute-start(bf16[4,128,128]{2,1,0:T(8,128)(2,1)S(1)} %shard_map.77.own_ref.dens_ref), channel_id=1, source_target_pairs={{2,0},{3,1},{4,2},{5,3},{6,4},{7,5},{8,6},{9,7},{10,8},{11,9},{12,... | collective-permute-start | bytes 393224 | tf_op jit(solution)/shard_map/ppermute | solution.py:37
  38.6 11.6 %collective-permute-start.2 = (bf16[4,128,128]{2,1,0:T(8,128)(2,1)S(1)}, bf16[4,128,128]{2,1,0:T(8,128)(2,1)S(1)}, u32[]{:S(2)}, u32[]{:S(2)}) collective-permute-start(bf16[4,128,128]{2,1,0:T(8,128)(2,1)S(1)} %shard_map.77.own_ref.dens_ref), channel_id=1, source_target_pairs={{14,0},{15,1},{0,2},{1,3},{2,4},{3,5},{4,6},{5,7},{6,8},{7,9},{8,1... | collective-permute-start | bytes 393224 | tf_op jit(solution)/shard_map/ppermute | solution.py:37
  38.7 15.4 %collective-permute-start.1 = (bf16[4,128,128]{2,1,0:T(8,128)(2,1)S(1)}, bf16[4,128,128]{2,1,0:T(8,128)(2,1)S(1)}, u32[]{:S(2)}, u32[]{:S(2)}) collective-permute-start(bf16[4,128,128]{2,1,0:T(8,128)(2,1)S(1)} %shard_map.77.own_ref.dens_ref), channel_id=1, source_target_pairs={{0,1},{1,0},{2,3},{3,2},{4,5},{5,4},{6,7},{7,6},{8,9},{9,8},{10,11... | collective-permute-start | bytes 393224 | tf_op jit(solution)/shard_map/ppermute | solution.py:227
  44.2 9.8 %collective-permute-start.5 = (bf16[4,128,128]{2,1,0:T(8,128)(2,1)S(1)}, bf16[4,128,128]{2,1,0:T(8,128)(2,1)S(1)}, u32[]{:S(2)}, u32[]{:S(2)}) collective-permute-start(bf16[4,128,128]{2,1,0:T(8,128)(2,1)S(1)} %collective-permute-done.3.refs_2_), channel_id=1, source_target_pairs={{0,1},{1,0},{2,3},{3,2},{4,5},{5,4},{6,7},{7,6},{8,9},{9,8},{10,11... | collective-permute-start | bytes 393224 | tf_op jit(solution)/shard_map/ppermute | solution.py:227
  47.7 7.3 %collective-permute-start = (bf16[8,128,128]{2,1,0:T(8,128)(2,1)S(1)}, bf16[8,128,128]{2,1,0:T(8,128)(2,1)S(1)}, u32[]{:S(2)}, u32[]{:S(2)}) collective-permute-start(bf16[8,128,128]{2,1,0:T(8,128)(2,1)S(1)} %all-to-all-done.2.mine_ref), channel_id=1, source_target_pairs={{0,1},{1,0},{2,3},{3,2},{4,5},{5,4},{6,7},{7,6},{8,9},{9,8},{10,11... | collective-permute-start | bytes 786440 | tf_op jit(solution)/shard_map/ppermute | solution.py:227
  50.3 4.8 %collective-permute-start.6 = (bf16[4,128,128]{2,1,0:T(8,128)(2,1)S(1)}, bf16[4,128,128]{2,1,0:T(8,128)(2,1)S(1)}, u32[]{:S(2)}, u32[]{:S(2)}) collective-permute-start(bf16[4,128,128]{2,1,0:T(8,128)(2,1)S(1)} %broadcast_select_fusion), channel_id=1, source_target_pairs={{0,15},{1,2},{2,1},{3,4},{4,3},{5,6},{6,5},{7,8},{8,7},{9,10},{10,... | collective-permute-start | bytes 393224 | tf_op jit(solution)/shard_map/ppermute | solution.py:232
  50.6 4.5 %collective-permute-start.4 = (bf16[4,128,128]{2,1,0:T(8,128)(2,1)S(1)}, bf16[4,128,128]{2,1,0:T(8,128)(2,1)S(1)}, u32[]{:S(2)}, u32[]{:S(2)}) collective-permute-start(bf16[4,128,128]{2,1,0:T(8,128)(2,1)S(1)} %collective-permute-done.2.refs_1_), channel_id=1, source_target_pairs={{0,1},{1,0},{2,3},{3,2},{4,5},{5,4},{6,7},{7,6},{8,9},{9,8},{10,11... | collective-permute-start | bytes 393224 | tf_op jit(solution)/shard_map/ppermute | solution.py:227

commit v4 on v3

--- a/solution.py
+++ b/solution.py
@@ -73,10 +73,13 @@
                 lo_ref[to, block * lanes : (block + 1) * lanes] = lo
 
 
-def transform_kernel(hi_ref, lo_ref, hist_ref, basis_ref, out_ref):
+def transform_kernel(hi_ref, lo_ref, hist_ref, basis_hbm, out_ref, basis_ref, sem):
+    copy = pltpu.make_async_copy(basis_hbm, basis_ref, sem)
+    copy.start()
     hist = hist_ref[...].reshape(STEPS, 128)
     total = nn(hi_ref[...], hist) + nn(lo_ref[...], hist)
     out_ref[...] = total.astype(BF16).reshape(out_ref.shape)
+    copy.wait()
 
 
 def signs(shape):
@@ -100,19 +103,21 @@
     return jnp.where(inner < limits, limits, 0.0), outer
 
 
-def table_kernel(info_ref, masked_hbm, hi_ref, lo_ref, base_c, base_s):
+def table_kernel(info_ref, hi_ref, lo_ref, base_c, base_s):
     fill_table(info_ref[5], hi_ref, lo_ref, base_c, base_s)
 
 
-def mask_kernel(info_ref, ranks_ref, couple_hbm, masked_hbm, couple_ref, masked_ref, sems):
+def mask_kernel(info_ref, ranks_hbm, couple_hbm, masked_ref, ranks_ref, couple_ref, sems):
+    rank_copy = pltpu.make_async_copy(ranks_hbm, ranks_ref, sems.at[4])
+    rank_copy.start()
     copies = [
-        pltpu.make_async_copy(couple_hbm.at[pl.ds(8 * group, 8)], couple_ref.at[group], sems.at[0, group])
+        pltpu.make_async_copy(couple_hbm.at[pl.ds(8 * group, 8)], couple_ref.at[group], sems.at[group])
         for group in range(4)
     ]
     for copy in copies:
         copy.start()
+    rank_copy.wait()
     limits, outer = mask_limits([info_ref[slot] for slot in range(4)], ranks_ref)
-    back = []
     for group in range(4):
         copies[group].wait()
         for wave in range(8):
@@ -120,29 +125,20 @@
             keep = outer < limits[at : at + 1]
             for part in range(2):
                 block = couple_ref[group, wave, part].astype(F32)
-                masked_ref[group, wave, part] = jnp.where(keep, block, 0.0).astype(BF16)
-        back.append(
-            pltpu.make_async_copy(masked_ref.at[group], masked_hbm.at[pl.ds(8 * group, 8)], sems.at[1, group])
-        )
-        back[-1].start()
-    for copy in back:
-        copy.wait()
-
-
-def dens_kernel(recv_ref, dens_ref):
+                masked_ref[at, part] = jnp.where(keep, block, 0.0).astype(BF16)
+
+
+def coeff_kernel(recv_ref, basis_ref, out_ref):
     rows = jnp.swapaxes(recv_ref[...].astype(F32), 0, 1).reshape(2, 32, 8, 128)
-    for group in range(4):
-        dens_ref[group] = rows[:, 8 * group : 8 * group + 8].reshape(128, 128).T.astype(BF16)
-
-
-def coeff_kernel(dens_ref, basis_ref, coef_ref):
     lane = lax.broadcasted_iota(jnp.int32, (32, 128), 1)
     lane_wave = (lane >> 3) & 7
     sign = signs((32, 128))
-    products = [
-        nn(basis_ref[8 * group : 8 * group + 8].reshape(512, 128), dens_ref[group]).reshape(8, 2, 32, 128)
-        for group in range(4)
-    ]
+    products = []
+    for group in range(4):
+        dens = rows[:, 8 * group : 8 * group + 8].reshape(128, 128).T.astype(BF16)
+        out_ref[group] = dens
+        left = basis_ref[8 * group : 8 * group + 8].reshape(512, 128)
+        products.append(nn(left, dens).reshape(8, 2, 32, 128))
     for group, out in enumerate(products):
         by_re = jnp.zeros((32, 128), F32)
         by_im = jnp.zeros((32, 128), F32)
@@ -150,8 +146,7 @@
             by_re = jnp.where(lane_wave == wave, out[wave, 0], by_re)
             by_im = jnp.where(lane_wave == wave, out[wave, 1], by_im)
         value = (by_re + sign * pltpu.roll(by_im, 64, 1)).astype(BF16)
-        for copy in range(coef_ref.shape[0]):
-            coef_ref[copy, group * 32 : (group + 1) * 32] = value
+        out_ref[4, group * 32 : (group + 1) * 32] = value
 
 
 def near_product(blocks, dens):
@@ -163,40 +158,64 @@
     return nn(jnp.concatenate(left, 1), jnp.concatenate(right, 0))
 
 
-def near_own_kernel(blocks_hbm, own_ref, basis_ref, out_ref, rest_ref, turned_ref, blocks_ref, sems):
+def near_own_kernel(
+    blocks_hbm, own_ref, basis_hbm, block_ref,
+    out_ref, rest_ref, turned_ref, blocks_ref, basis_ref, sems,
+):
     copies = [
         pltpu.make_async_copy(blocks_hbm.at[0, pl.ds(8 * group, 8)], blocks_ref.at[group], sems.at[group])
         for group in range(4)
     ]
     rest = pltpu.make_async_copy(blocks_hbm.at[pl.ds(1, 3)], rest_ref, sems.at[4])
+    bases = pltpu.make_async_copy(basis_hbm, basis_ref, sems.at[5])
     for copy in copies:
         copy.start()
+    bases.start()
     rest.start()
+    for group in range(4):
+        copies[group].wait()
+        out_ref[group] = near_product(blocks_ref[group], own_ref[group])
+    bases.wait()
     for group in range(4):
         for part in range(2):
             basis = basis_ref[8 * group : 8 * group + 8, part].reshape(256, 128)
             turned_ref[group, :, part * 256 : (part + 1) * 256] = basis.astype(F32).T.astype(BF16)
-    for group in range(4):
-        copies[group].wait()
-        out_ref[group] = near_product(blocks_ref[group], own_ref[group])
     rest.wait()
 
 
-def final_kernel(info_ref, blocks_ref, first_ref, mine_ref, other_ref, couple_ref, turned_ref, *refs):
-    moved_refs, out_ref = refs[:-1], refs[-1]
+def forward_kernel(info_ref, own_ref, behind_ref, ahead_ref, masked_ref, block_ref, picked_ref):
+    block_ref[0] = own_ref[4]
+    block_ref[1] = behind_ref[4]
+    block_ref[2] = ahead_ref[4]
+    picked_ref[...] = jnp.where((info_ref[4] & 1) == 1, behind_ref[:4], ahead_ref[:4])
+
+
+def join_kernel(up_ref, down_ref, turned_ref, beyond_ref, out_ref):
+    out_ref[0:3] = up_ref[...]
+    out_ref[3:5] = down_ref[0:2]
+
+
+def final_kernel(info_ref, blocks_ref, first_ref, couple_ref, turned_ref, own_ref, *refs):
+    moved_refs, (up_ref, down_ref, joined_ref, out_ref, all_ref) = refs[:6], refs[6:]
+    beside_ref, behind_ref, ahead_ref, other_behind_ref, other_ahead_ref = moved_refs[:5]
     me = info_ref[4]
     even_core = (me & 1) == 0
+    chip, core = me >> 1, me & 1
+    held = [
+        (core, own_ref, behind_ref, ahead_ref, up_ref, down_ref, 0),
+        (1 - core, beside_ref, other_behind_ref, other_ahead_ref, joined_ref, joined_ref, 3),
+    ]
+    for lane, at_chip, before, after, up, down, base in held:
+        parts = [(0, at_chip, 4), (-1, before, 4), (1, after, 4), (-3, up, 0), (-4, up, 1), (-2, up, 2), (3, down, base), (2, down, base + 1)]
+        for away, ref, index in parts:
+            all_ref[(chip + away) & 7, lane] = ref[index]
     row_wave = lax.broadcasted_iota(jnp.int32, (8, 32, 128), 0)
     lane_wave = (lax.broadcasted_iota(jnp.int32, (8, 32, 128), 2) >> 3) & 7
     same = (row_wave == lane_wave).reshape(256, 128)
     sign = signs((256, 128))
     products = []
     for group in range(4):
-        mine = mine_ref[:, group * 32 : (group + 1) * 32]
-        other = other_ref[:, group * 32 : (group + 1) * 32]
-        evens = jnp.where(even_core, mine, other)
-        odds = jnp.where(even_core, other, mine)
-        right = jnp.stack([evens, odds], 1).reshape(512, 128)
+        right = all_ref[:, :, group * 32 : (group + 1) * 32].reshape(512, 128)
         left = couple_ref[8 * group : 8 * group + 8].reshape(512, 512)
         products.append(nn(left, right).reshape(8, 2, 32, 128))
     pairs = []
@@ -254,42 +273,58 @@
     vmem = pl.BlockSpec(memory_space=VMEM)
     hbm = pl.BlockSpec(memory_space=pltpu.HBM)
     groups = [list(range(8)), list(range(8, 16))]
-    cores = [[2 * z + core for z in range(8)] for core in range(2)]
-
+
+    dma = pltpu.SemaphoreType.DMA
+    couple, blocks_hbm, ranks_hbm, outer, inner = [
+        pltpu.with_memory_space_constraint(a, pltpu.HBM)
+        for a in (coupling[0], near_blocks[0], ranks[0].T, basis_out, basis_in)
+    ]
     packed = call(pack_kernel, shape((16, 64, 128), BF16), [vmem])(history)
     steps = lax.all_to_all(packed, "freq", 0, 0, tiled=True)
-    couple, blocks_hbm = [pltpu.with_memory_space_constraint(a, pltpu.HBM) for a in (coupling[0], near_blocks[0])]
-    dma = pltpu.SemaphoreType.DMA
     masked = call(
         mask_kernel,
-        pltpu.HBM((32, 2, 32, 512), BF16),
-        [smem, vmem, hbm],
-        [VMEM((4, 8, 2, 32, 512), BF16), VMEM((4, 8, 2, 32, 512), BF16), dma((2, 4))],
-        hbm,
-    )(info, ranks[0].T, couple)
+        shape((32, 2, 32, 512), BF16),
+        [smem, hbm, hbm],
+        [VMEM((16, 32), jnp.int32), VMEM((4, 8, 2, 32, 512), BF16), dma((5,))],
+    )(info, ranks_hbm, couple)
     hi, lo = call(
-        table_kernel, [shape((512, STEPS), BF16)] * 2, [smem, hbm], [VMEM((256, 128), F32)] * 2
-    )(info, pltpu.with_memory_space_constraint(masked, pltpu.HBM))
-    spectrum = call(transform_kernel, shape((8, 64, 128), BF16), [vmem] * 4)(hi, lo, steps, basis_in)
+        table_kernel, [shape((512, STEPS), BF16)] * 2, [smem], [VMEM((256, 128), F32)] * 2
+    )(info)
+    spectrum, bases = call(
+        transform_kernel,
+        [shape((8, 64, 128), BF16), shape((32, 2, 32, 128), BF16)],
+        [vmem] * 3 + [hbm],
+        [dma],
+    )(hi, lo, steps, inner)
     received = lax.all_to_all(spectrum, "freq", 0, 0, tiled=True, axis_index_groups=groups)
-    dens = call(dens_kernel, shape((4, 128, 128), BF16), [vmem])(received)
-    beside = partner(dens)
-    behind = from_behind(dens, "clus", 2)
-    ahead = from_behind(dens, "clus", -2)
-    coeffs = call(coeff_kernel, shape((8, 128, 128), BF16), [vmem] * 2)(dens, basis_in)
-    same_core = lax.all_to_all(coeffs, "clus", 0, 0, tiled=True, axis_index_groups=cores)
-    beyond = cross(jnp.where((me & 1) == 1, behind, ahead))
+    packet = call(coeff_kernel, shape((5, 128, 128), BF16), [vmem] * 2)(received, bases)
+    beside = partner(packet)
+    behind = from_behind(packet, "clus", 2)
+    ahead = from_behind(packet, "clus", -2)
+    block, picked = call(
+        forward_kernel, [shape((3, 128, 128), BF16), shape((4, 128, 128), BF16)], [smem] + [vmem] * 4
+    )(info, packet, behind, ahead, masked)
+    up = from_behind(block, "clus", 6)
+    down = from_behind(block, "clus", -6)
+    beyond = cross(picked)
     first, rest, turned = call(
         near_own_kernel,
-        [shape((4, 256, 128), F32), shape((3, 32, 2, 128, 128), BF16), shape((4, 128, 512), BF16)],
-        [hbm] + [vmem] * 2,
-        [VMEM((4, 8, 2, 128, 128), BF16), dma((5,))],
-    )(blocks_hbm, dens, basis_out)
-    moved = [beside, behind, ahead, partner(behind), partner(ahead), beyond]
-    other_core = partner(same_core)
-    out = call(final_kernel, shape((32, 16, 128), BF16), [smem] + [vmem] * 12)(
-        info, rest, first, same_core, other_core, masked, turned, *moved
-    )
+        [
+            shape((4, 256, 128), F32),
+            shape((3, 32, 2, 128, 128), BF16),
+            shape((4, 128, 512), BF16),
+        ],
+        [hbm, vmem, hbm, vmem],
+        [VMEM((4, 8, 2, 128, 128), BF16), VMEM((32, 2, 32, 128), BF16), dma((6,))],
+    )(blocks_hbm, packet, outer, block)
+    joined = call(join_kernel, shape((5, 128, 128), BF16), [vmem] * 4)(up, down, turned, beyond)
+    moved = [beside, behind, ahead, partner(behind), partner(ahead), beyond, up, down, partner(joined)]
+    out = call(
+        final_kernel,
+        shape((32, 16, 128), BF16),
+        [smem] + [vmem] * 14,
+        [VMEM((8, 2, 128, 128), BF16)],
+    )(info, rest, first, masked, turned, packet, *moved)
     return out.reshape(32, 2, 8, 128)
 
 

time: 59.6 us -> 59.9 us (level)
  the two profiles are of different devices: /device:TPU:1 before, /device:TPU:33 now
where the time goes in v4:
time: 59.9 us; the launch traced here: 59.6 us
  starting transfers between devices  21.7 us (36%)
  Pallas kernels  14.9 us (25%)
  waiting for transfers between devices  13.8 us (23%)
  blocking collectives  7.89 us (13%)
  local copies, waits for them, and re-layouts  1.11 us (2%)
    all_to_all x1, blocking collectives, local(): lax.all_to_all(spectrum, 'freq', 0, 0, tiled=True, axis_index_groups=groups)  7.89 us
    ppermute x4, waiting for transfers between devices, from_behind(): return lax.ppermute(block, axis, route)  7.57 us
    ppermute x1, starting transfers between devices, cross(): lax.ppermute(block, 'clus', [(i, (i + 1 if i % 2 else i - 1) % size) for...  7.21 us
    all_to_all x1, starting transfers between devices, local(): steps = lax.all_to_all(packed, 'freq', 0, 0, tiled=True)  6.75 us
    ppermute x4, starting transfers between devices, from_behind(): return lax.ppermute(block, axis, route)  6.19 us
    all_to_all x1, waiting for transfers between devices, local(): steps = lax.all_to_all(packed, 'freq', 0, 0, tiled=True)  5.21 us
    pallas_call x1, Pallas kernels, local(): call(final_kernel, shape((32, 16, 128), BF16), [smem] + [vmem] * 14, [VME...  4.22 us
    pallas_call x1, Pallas kernels, local(): call(near_own_kernel, [shape((4, 256, 128), F32), shape((3, 32, 2, 128, 1...  3.65 us
  transfers between devices with their start and end apart: 10, of which 6 were waited for; matrix products, arithmetic and copies ran while one was open for 0% of the time, Pallas kernels for 13%

profile of v4, /device:TPU:33, one launch (start us, length us, event | category | flops | bytes accessed | tf_op | source)
XLA Modules:
  0.0 59.6 jit_solution(5128291104712626860)
XLA Ops:
  0.0 0.9 %copy-done.1 = bf16[64,8,128]{2,1,0:T(8,128)(2,1)S(1)} copy-done((bf16[64,8,128]{2,1,0:T(8,128)(2,1)S(1)}, bf16[64,8,128]{2,1,0:T(8,128)(2,1)}, u32[]{:S(2)}) %copy-start.1) | copy-done | bytes 131096
  0.9 0.8 %shard_map.74 = bf16[16,64,128]{2,1,0:T(8,128)(2,1)} custom-call(bf16[64,8,128]{2,1,0:T(8,128)(2,1)S(1)} %copy-done.1), custom_call_target="tpu_custom_call" | custom-call | tf_op jit(solution)/shard_map/pallas_call | solution.py:282
  1.7 6.8 %all-to-all-start = ((bf16[16,64,128]{2,1,0:T(8,128)(2,1)}), bf16[16,64,128]{2,1,0:T(8,128)(2,1)S(1)}, u32[]{:S(2)}, u32[]{:S(2)}) async-start(bf16[16,64,128]{2,1,0:T(8,128)(2,1)} %shard_map.74), calls=%async_computation | async-start | bytes 524288 | tf_op jit(solution)/shard_map/all_to_all | solution.py:283
  8.5 0.2 dynamic-slice_reduce_fusion
  8.7 2.0 %shard_map.73 = (bf16[512,1024]{1,0:T(8,128)(2,1)S(1)}, bf16[512,1024]{1,0:T(8,128)(2,1)S(1)}) custom-call(s32[6]{0:T(128)S(1)} %pad_add_fusion.info_ref), custom_call_target="tpu_custom_call" | custom-call | tf_op jit(solution)/shard_map/pallas_call | solution.py:290
  10.7 5.2 %all-to-all-done.hist_ref = bf16[16,64,128]{2,1,0:T(8,128)(2,1)S(1)} async-done(((bf16[16,64,128]{2,1,0:T(8,128)(2,1)}), bf16[16,64,128]{2,1,0:T(8,128)(2,1)S(1)}, u32[]{:S(2)}, u32[]{:S(2)}) %all-to-all-start) | async-done | bytes 262176 | tf_op jit(solution)/shard_map/all_to_all | solution.py:283
  15.9 1.1 %shard_map.75 = (bf16[8,64,128]{2,1,0:T(8,128)(2,1)S(1)}, bf16[32,2,32,128]{3,2,1,0:T(8,128)(2,1)S(1)}) custom-call(bf16[512,1024]{1,0:T(8,128)(2,1)S(1)} %get-tuple-element.14.hi_ref, bf16[512,1024]{1,0:T(8,128)(2,1)S(1)} %get-tuple-element.15.lo_ref, bf16[16,64,128]{2,1,0:T(8,128)(2,1)S(1)} %all-to-all-done.hist_ref, bf16[32,2,32,128]{3,2,1,0:T(8,128)(2,1)} %basis_hbm.2), custom_call_target="tpu_custom_call" | custom-call | tf_op jit(solution)/shard_map/pallas_call | solution.py:293
  17.0 7.9 %all_to_all.10.recv_ref = bf16[8,64,128]{2,1,0:T(8,128)(2,1)S(1)} all-to-all(bf16[8,64,128]{2,1,0:T(8,128)(2,1)S(1)} %get-tuple-element.16), channel_id=1, replica_groups={{0,16,32,48,64,80,96,112},{128,144,160,176,192,208,224,240},{1,17,33,49..., dimensions={0} | all-to-all | bytes 262144 | tf_op jit(solution)/shard_map/all_to_all | solution.py:299
  24.9 0.5 shard_map.76.own_ref
  25.3 1.7 %collective-permute-start = (bf16[5,128,128]{2,1,0:T(8,128)(2,1)S(1)}, bf16[5,128,128]{2,1,0:T(8,128)(2,1)S(1)}, u32[]{:S(2)}, u32[]{:S(2)}) collective-permute-start(bf16[5,128,128]{2,1,0:T(8,128)(2,1)S(1)} %shard_map.76.own_ref), channel_id=1, source_target_pairs={{14,0},{15,1},{0,2},{1,3},{2,4},{3,5},{4,6},{5,7},{6,8},{7,9},{8,1... | collective-permute-start | bytes 491528 | tf_op jit(solution)/shard_map/ppermute | solution.py:37
  27.0 2.2 %shard_map.77.masked_ref.couple_ref = bf16[32,2,32,512]{3,2,1,0:T(8,128)(2,1)S(1)} custom-call(s32[6]{0:T(128)S(1)} %pad_add_fusion.info_ref, s32[16,32]{1,0:T(8,128)} %bitcast.10, bf16[32,2,32,512]{3,2,1,0:T(8,128)(2,1)} %bitcast.9), custom_call_target="tpu_custom_call" | custom-call | tf_op jit(solution)/shard_map/pallas_call | solution.py:284
  29.3 0.3 collective-permute-done.behind_ref.refs_1_
  29.6 1.8 %collective-permute-done.1.ahead_ref.refs_2_ = bf16[5,128,128]{2,1,0:T(8,128)(2,1)S(1)} collective-permute-done((bf16[5,128,128]{2,1,0:T(8,128)(2,1)S(1)}, bf16[5,128,128]{2,1,0:T(8,128)(2,1)S(1)}, u32[]{:S(2)}, u32[]{:S(2)}) %collective-permute-start.1) | collective-permute-done | bytes 163872 | tf_op jit(solution)/shard_map/ppermute | solution.py:37
  31.4 0.6 shard_map.78
  32.0 7.2 %collective-permute-start.5 = (bf16[4,128,128]{2,1,0:T(8,128)(2,1)S(1)}, bf16[4,128,128]{2,1,0:T(8,128)(2,1)S(1)}, u32[]{:S(2)}, u32[]{:S(2)}) collective-permute-start(bf16[4,128,128]{2,1,0:T(8,128)(2,1)S(1)} %get-tuple-element.22), channel_id=1, source_target_pairs={{0,15},{1,2},{2,1},{3,4},{4,3},{5,6},{6,5},{7,8},{8,7},{9,10},{10,... | collective-permute-start | bytes 393224 | tf_op jit(solution)/shard_map/ppermute | solution.py:251
  39.2 2.7 %collective-permute-start.6 = (bf16[3,128,128]{2,1,0:T(8,128)(2,1)S(1)}, bf16[3,128,128]{2,1,0:T(8,128)(2,1)S(1)}, u32[]{:S(2)}, u32[]{:S(2)}) collective-permute-start(bf16[3,128,128]{2,1,0:T(8,128)(2,1)S(1)} %get-tuple-element.18.block_ref), channel_id=1, source_target_pairs={{10,0},{11,1},{12,2},{13,3},{14,4},{15,5},{0,6},{1,7},{2,8},{3,9},... | collective-permute-start | bytes 294920 | tf_op jit(solution)/shard_map/ppermute | solution.py:37
  41.8 1.8 %collective-permute-start.7 = (bf16[3,128,128]{2,1,0:T(8,128)(2,1)S(1)}, bf16[3,128,128]{2,1,0:T(8,128)(2,1)S(1)}, u32[]{:S(2)}, u32[]{:S(2)}) collective-permute-start(bf16[3,128,128]{2,1,0:T(8,128)(2,1)S(1)} %get-tuple-element.18.block_ref), channel_id=1, source_target_pairs={{6,0},{7,1},{8,2},{9,3},{10,4},{11,5},{12,6},{13,7},{14,8},{15,9},... | collective-permute-start | bytes 294920 | tf_op jit(solution)/shard_map/ppermute | solution.py:37
  43.7 3.7 %shard_map.79 = (f32[4,256,128]{2,1,0:T(8,128)S(1)}, bf16[3,32,2,128,128]{4,3,2,1,0:T(8,128)(2,1)S(1)}, bf16[4,128,512]{2,1,0:T(8,128)(2,1)S(1)}) custom-call(bf16[4,32,2,128,128]{4,3,2,1,0:T(8,128)(2,1)} %bitcast.8, bf16[5,128,128]{2,1,0:T(8,128)(2,1)S(1)} %shard_map.76.own_ref, bf16[32,2,32,128]{3,2,1,0:T(8,128)(2,1)} %basis_hbm.3, ...), custom_call_target="tpu_custom_call" | custom-call | tf_op jit(solution)/shard_map/pallas_call | solution.py:310
  47.3 0.6 collective-permute-start.3
  47.9 2.1 %collective-permute-done.6.up_ref.refs_6_ = bf16[3,128,128]{2,1,0:T(8,128)(2,1)S(1)} collective-permute-done((bf16[3,128,128]{2,1,0:T(8,128)(2,1)S(1)}, bf16[3,128,128]{2,1,0:T(8,128)(2,1)S(1)}, u32[]{:S(2)}, u32[]{:S(2)}) %collective-permute-start.6) | collective-permute-done | bytes 98336 | tf_op jit(solution)/shard_map/ppermute | solution.py:37
  50.0 3.4 %collective-permute-done.7.down_ref.refs_7_ = bf16[3,128,128]{2,1,0:T(8,128)(2,1)S(1)} collective-permute-done((bf16[3,128,128]{2,1,0:T(8,128)(2,1)S(1)}, bf16[3,128,128]{2,1,0:T(8,128)(2,1)S(1)}, u32[]{:S(2)}, u32[]{:S(2)}) %collective-permute-start.7) | collective-permute-done | bytes 98336 | tf_op jit(solution)/shard_map/ppermute | solution.py:37
  53.4 1.0 %collective-permute-start.8 = (bf16[5,128,128]{2,1,0:T(8,128)(2,1)S(1)}, bf16[5,128,128]{2,1,0:T(8,128)(2,1)S(1)}, u32[]{:S(2)}, u32[]{:S(2)}) collective-permute-start(bf16[5,128,128]{2,1,0:T(8,128)(2,1)S(1)} %shard_map.80), channel_id=1, source_target_pairs={{0,1},{1,0},{2,3},{3,2},{4,5},{5,4},{6,7},{7,6},{8,9},{9,8},{10,11... | collective-permute-start | bytes 491528 | tf_op jit(solution)/shard_map/ppermute | solution.py:246
  54.4 1.0 %collective-permute-done.8.refs_8_ = bf16[5,128,128]{2,1,0:T(8,128)(2,1)S(1)} collective-permute-done((bf16[5,128,128]{2,1,0:T(8,128)(2,1)S(1)}, bf16[5,128,128]{2,1,0:T(8,128)(2,1)S(1)}, u32[]{:S(2)}, u32[]{:S(2)}) %collective-permute-start.8) | collective-permute-done | bytes 163872 | tf_op jit(solution)/shard_map/ppermute | solution.py:246
  55.4 4.2 %shard_map.81 = bf16[32,16,128]{2,1,0:T(8,128)(2,1)} custom-call(s32[6]{0:T(128)S(1)} %pad_add_fusion.info_ref, bf16[3,32,2,128,128]{4,3,2,1,0:T(8,128)(2,1)S(1)} %get-tuple-element.19.blocks_ref, f32[4,256,128]{2,1,0:T(8,128)S(1)} %get-tuple-element.20.first_ref, bf16[32,2,32,512]{3,2,1,0:T(8,128)(2,1)S(1)} %shard_map.77.masked_ref.couple_ref, ...), custom_call_target="tpu_custom_call" | custom-call | tf_op jit(solution)/shard_map/pallas_call | solution.py:322
  (12 shorter events, 0.1 us)
Async XLA Ops:
  0.0 8.5 %copy-start = (s32[16,4]{0,1:T(4,128)S(1)}, s32[16,4]{0,1:T(4,128)}, u32[]{:S(2)}) copy-start(s32[16,4]{0,1:T(4,128)} %param.9) | copy-start | bytes 772
  0.0 0.9 %copy-start.1 = (bf16[64,8,128]{2,1,0:T(8,128)(2,1)S(1)}, bf16[64,8,128]{2,1,0:T(8,128)(2,1)}, u32[]{:S(2)}) copy-start(bf16[64,8,128]{2,1,0:T(8,128)(2,1)} %hist_ref.1) | copy-start | bytes 393220
  1.7 14.2 %all-to-all-start = ((bf16[16,64,128]{2,1,0:T(8,128)(2,1)}), bf16[16,64,128]{2,1,0:T(8,128)(2,1)S(1)}, u32[]{:S(2)}, u32[]{:S(2)}) async-start(bf16[16,64,128]{2,1,0:T(8,128)(2,1)} %shard_map.74), calls=%async_computation | async-start | bytes 524288 | tf_op jit(solution)/shard_map/all_to_all | solution.py:283
  25.3 4.2 %collective-permute-start = (bf16[5,128,128]{2,1,0:T(8,128)(2,1)S(1)}, bf16[5,128,128]{2,1,0:T(8,128)(2,1)S(1)}, u32[]{:S(2)}, u32[]{:S(2)}) collective-permute-start(bf16[5,128,128]{2,1,0:T(8,128)(2,1)S(1)} %shard_map.76.own_ref), channel_id=1, source_target_pairs={{14,0},{15,1},{0,2},{1,3},{2,4},{3,5},{4,6},{5,7},{6,8},{7,9},{8,1... | collective-permute-start | bytes 491528 | tf_op jit(solution)/shard_map/ppermute | solution.py:37
  27.0 4.3 %collective-permute-start.1 = (bf16[5,128,128]{2,1,0:T(8,128)(2,1)S(1)}, bf16[5,128,128]{2,1,0:T(8,128)(2,1)S(1)}, u32[]{:S(2)}, u32[]{:S(2)}) collective-permute-start(bf16[5,128,128]{2,1,0:T(8,128)(2,1)S(1)} %shard_map.76.own_ref), channel_id=1, source_target_pairs={{2,0},{3,1},{4,2},{5,3},{6,4},{7,5},{8,6},{9,7},{10,8},{11,9},{12,... | collective-permute-start | bytes 491528 | tf_op jit(solution)/shard_map/ppermute | solution.py:37
  32.0 21.4 %collective-permute-start.5 = (bf16[4,128,128]{2,1,0:T(8,128)(2,1)S(1)}, bf16[4,128,128]{2,1,0:T(8,128)(2,1)S(1)}, u32[]{:S(2)}, u32[]{:S(2)}) collective-permute-start(bf16[4,128,128]{2,1,0:T(8,128)(2,1)S(1)} %get-tuple-element.22), channel_id=1, source_target_pairs={{0,15},{1,2},{2,1},{3,4},{4,3},{5,6},{6,5},{7,8},{8,7},{9,10},{10,... | collective-permute-start | bytes 393224 | tf_op jit(solution)/shard_map/ppermute | solution.py:251
  39.2 10.8 %collective-permute-start.6 = (bf16[3,128,128]{2,1,0:T(8,128)(2,1)S(1)}, bf16[3,128,128]{2,1,0:T(8,128)(2,1)S(1)}, u32[]{:S(2)}, u32[]{:S(2)}) collective-permute-start(bf16[3,128,128]{2,1,0:T(8,128)(2,1)S(1)} %get-tuple-element.18.block_ref), channel_id=1, source_target_pairs={{10,0},{11,1},{12,2},{13,3},{14,4},{15,5},{0,6},{1,7},{2,8},{3,9},... | collective-permute-start | bytes 294920 | tf_op jit(solution)/shard_map/ppermute | solution.py:37
  41.8 11.5 %collective-permute-start.7 = (bf16[3,128,128]{2,1,0:T(8,128)(2,1)S(1)}, bf16[3,128,128]{2,1,0:T(8,128)(2,1)S(1)}, u32[]{:S(2)}, u32[]{:S(2)}) collective-permute-start(bf16[3,128,128]{2,1,0:T(8,128)(2,1)S(1)} %get-tuple-element.18.block_ref), channel_id=1, source_target_pairs={{6,0},{7,1},{8,2},{9,3},{10,4},{11,5},{12,6},{13,7},{14,8},{15,9},... | collective-permute-start | bytes 294920 | tf_op jit(solution)/shard_map/ppermute | solution.py:37
  43.7 10.7 %collective-permute-start.2 = (bf16[5,128,128]{2,1,0:T(8,128)(2,1)S(1)}, bf16[5,128,128]{2,1,0:T(8,128)(2,1)S(1)}, u32[]{:S(2)}, u32[]{:S(2)}) collective-permute-start(bf16[5,128,128]{2,1,0:T(8,128)(2,1)S(1)} %shard_map.76.own_ref), channel_id=1, source_target_pairs={{0,1},{1,0},{2,3},{3,2},{4,5},{5,4},{6,7},{7,6},{8,9},{9,8},{10,11... | collective-permute-start | bytes 491528 | tf_op jit(solution)/shard_map/ppermute | solution.py:246
  47.3 7.1 %collective-permute-start.3 = (bf16[5,128,128]{2,1,0:T(8,128)(2,1)S(1)}, bf16[5,128,128]{2,1,0:T(8,128)(2,1)S(1)}, u32[]{:S(2)}, u32[]{:S(2)}) collective-permute-start(bf16[5,128,128]{2,1,0:T(8,128)(2,1)S(1)} %collective-permute-done.behind_ref.refs_1_), channel_id=1, source_target_pairs={{0,1},{1,0},{2,3},{3,2},{4,5},{5,4},{6,7},{7,6},{8,9},{9,8},{10,11... | collective-permute-start | bytes 491528 | tf_op jit(solution)/shard_map/ppermute | solution.py:246
  50.0 4.4 %collective-permute-start.4 = (bf16[5,128,128]{2,1,0:T(8,128)(2,1)S(1)}, bf16[5,128,128]{2,1,0:T(8,128)(2,1)S(1)}, u32[]{:S(2)}, u32[]{:S(2)}) collective-permute-start(bf16[5,128,128]{2,1,0:T(8,128)(2,1)S(1)} %collective-permute-done.1.ahead_ref.refs_2_), channel_id=1, source_target_pairs={{0,1},{1,0},{2,3},{3,2},{4,5},{5,4},{6,7},{7,6},{8,9},{9,8},{10,11... | collective-permute-start | bytes 491528 | tf_op jit(solution)/shard_map/ppermute | solution.py:246
  53.4 2.0 %collective-permute-start.8 = (bf16[5,128,128]{2,1,0:T(8,128)(2,1)S(1)}, bf16[5,128,128]{2,1,0:T(8,128)(2,1)S(1)}, u32[]{:S(2)}, u32[]{:S(2)}) collective-permute-start(bf16[5,128,128]{2,1,0:T(8,128)(2,1)S(1)} %shard_map.80), channel_id=1, source_target_pairs={{0,1},{1,0},{2,3},{3,2},{4,5},{5,4},{6,7},{7,6},{8,9},{9,8},{10,11... | collective-permute-start | bytes 491528 | tf_op jit(solution)/shard_map/ppermute | solution.py:246

commit v5 on v3

--- a/solution.py
+++ b/solution.py
@@ -104,13 +104,16 @@
     fill_table(info_ref[5], hi_ref, lo_ref, base_c, base_s)
 
 
-def mask_kernel(info_ref, ranks_ref, couple_hbm, masked_hbm, couple_ref, masked_ref, sems):
+def mask_kernel(info_ref, ranks_hbm, couple_hbm, masked_hbm, ranks_ref, couple_ref, masked_ref, sems, rank_sem):
+    rank_copy = pltpu.make_async_copy(ranks_hbm, ranks_ref, rank_sem)
+    rank_copy.start()
     copies = [
         pltpu.make_async_copy(couple_hbm.at[pl.ds(8 * group, 8)], couple_ref.at[group], sems.at[0, group])
         for group in range(4)
     ]
     for copy in copies:
         copy.start()
+    rank_copy.wait()
     limits, outer = mask_limits([info_ref[slot] for slot in range(4)], ranks_ref)
     back = []
     for group in range(4):
@@ -258,15 +261,23 @@
 
     packed = call(pack_kernel, shape((16, 64, 128), BF16), [vmem])(history)
     steps = lax.all_to_all(packed, "freq", 0, 0, tiled=True)
-    couple, blocks_hbm = [pltpu.with_memory_space_constraint(a, pltpu.HBM) for a in (coupling[0], near_blocks[0])]
+    couple, blocks_hbm, ranks_hbm = [
+        pltpu.with_memory_space_constraint(a, pltpu.HBM) for a in (coupling[0], near_blocks[0], ranks[0].T)
+    ]
     dma = pltpu.SemaphoreType.DMA
     masked = call(
         mask_kernel,
         pltpu.HBM((32, 2, 32, 512), BF16),
-        [smem, vmem, hbm],
-        [VMEM((4, 8, 2, 32, 512), BF16), VMEM((4, 8, 2, 32, 512), BF16), dma((2, 4))],
+        [smem, hbm, hbm],
+        [
+            VMEM((16, 32), jnp.int32),
+            VMEM((4, 8, 2, 32, 512), BF16),
+            VMEM((4, 8, 2, 32, 512), BF16),
+            dma((2, 4)),
+            dma,
+        ],
         hbm,
-    )(info, ranks[0].T, couple)
+    )(info, ranks_hbm, couple)
     hi, lo = call(
         table_kernel, [shape((512, STEPS), BF16)] * 2, [smem, hbm], [VMEM((256, 128), F32)] * 2
     )(info, pltpu.with_memory_space_constraint(masked, pltpu.HBM))

time: 59.6 us -> 59.1 us (level)
  local copies, waits for them, and re-layouts: 1.89 us -> 1.19 us
    unnamed x12 -> x10, local copies, waits for them, and re-layouts: 1.7 us -> 1 us
  transfers between devices with their start and end apart: 9 -> 9, of which waited for: 3 -> 3; matrix products, arithmetic and copies ran while one was open for 0% -> 0% of each run, Pallas kernels for 14% -> 15%
where the time goes in v5:
time: 59.1 us; the launch traced here: 58.7 us
  starting transfers between devices  28.2 us (48%)
  Pallas kernels  15.6 us (26%)
  blocking collectives  8.64 us (15%)
  waiting for transfers between devices  4.85 us (8%)
  local copies, waits for them, and re-layouts  1.19 us (2%)
    ppermute x4, starting transfers between devices, partner(): return lax.ppermute(block, 'clus', [(i, i ^ 1) for i in range(size)])  9.52 us
    all_to_all x1, blocking collectives, local(): lax.all_to_all(spectrum, 'freq', 0, 0, tiled=True, axis_index_groups=groups)  8.64 us
    all_to_all x1, starting transfers between devices, local(): lax.all_to_all(coeffs, 'clus', 0, 0, tiled=True, axis_index_groups=cores)  8.19 us
    all_to_all x1, starting transfers between devices, local(): steps = lax.all_to_all(packed, 'freq', 0, 0, tiled=True)  7.58 us
    pallas_call x1, Pallas kernels, local(): call(final_kernel, shape((32, 16, 128), BF16), [smem] + [vmem] * 12)  4.09 us
    pallas_call x1, Pallas kernels, local(): call(near_own_kernel, [shape((4, 256, 128), F32), shape((3, 32, 2, 128, 1...  3.49 us
    pallas_call x1, Pallas kernels, local(): call(mask_kernel, pltpu.HBM((32, 2, 32, 512), BF16), [smem, hbm, hbm], [V...  3.42 us
    ppermute x2, starting transfers between devices, from_behind(): return lax.ppermute(block, axis, route)  2.68 us
  transfers between devices with their start and end apart: 9, of which 3 were waited for; matrix products, arithmetic and copies ran while one was open for 0% of the time, Pallas kernels for 15%

profile of v5, /device:TPU:1, one launch (start us, length us, event | category | flops | bytes accessed | tf_op | source)
XLA Modules:
  0.0 58.7 jit_solution(4460667425434361040)
XLA Ops:
  0.0 1.0 %copy-done.4 = bf16[64,8,128]{2,1,0:T(8,128)(2,1)S(1)} copy-done((bf16[64,8,128]{2,1,0:T(8,128)(2,1)S(1)}, bf16[64,8,128]{2,1,0:T(8,128)(2,1)}, u32[]{:S(2)}) %copy-start.4) | copy-done | bytes 131096
  1.0 0.8 %shard_map.75 = bf16[16,64,128]{2,1,0:T(8,128)(2,1)} custom-call(bf16[64,8,128]{2,1,0:T(8,128)(2,1)S(1)} %copy-done.4), custom_call_target="tpu_custom_call" | custom-call | tf_op jit(solution)/shard_map/pallas_call | solution.py:262
  1.8 7.6 %all-to-all-start = ((bf16[16,64,128]{2,1,0:T(8,128)(2,1)}), bf16[16,64,128]{2,1,0:T(8,128)(2,1)S(1)}, u32[]{:S(2)}, u32[]{:S(2)}) async-start(bf16[16,64,128]{2,1,0:T(8,128)(2,1)} %shard_map.75), calls=%async_computation | async-start | bytes 524288 | tf_op jit(solution)/shard_map/all_to_all | solution.py:263
  9.4 0.2 dynamic-slice_reduce_fusion
  9.6 0.1 pad_add_fusion.info_ref
  9.7 3.4 %shard_map.73.masked_hbm.couple_ref = bf16[32,2,32,512]{3,2,1,0:T(8,128)(2,1)} custom-call(s32[6]{0:T(128)S(1)} %pad_add_fusion.info_ref, s32[16,32]{1,0:T(8,128)} %bitcast.10, bf16[32,2,32,512]{3,2,1,0:T(8,128)(2,1)} %bitcast.9), custom_call_target="tpu_custom_call" | custom-call | tf_op jit(solution)/shard_map/pallas_call | solution.py:268
  13.1 2.0 %shard_map.74 = (bf16[512,1024]{1,0:T(8,128)(2,1)S(1)}, bf16[512,1024]{1,0:T(8,128)(2,1)S(1)}) custom-call(s32[6]{0:T(128)S(1)} %pad_add_fusion.info_ref, bf16[32,2,32,512]{3,2,1,0:T(8,128)(2,1)} %shard_map.73.masked_hbm.couple_ref), custom_call_target="tpu_custom_call" | custom-call | tf_op jit(solution)/shard_map/pallas_call | solution.py:281
  15.0 1.8 %all-to-all-done.hist_ref = bf16[16,64,128]{2,1,0:T(8,128)(2,1)S(1)} async-done(((bf16[16,64,128]{2,1,0:T(8,128)(2,1)}), bf16[16,64,128]{2,1,0:T(8,128)(2,1)S(1)}, u32[]{:S(2)}, u32[]{:S(2)}) %all-to-all-start) | async-done | bytes 262176 | tf_op jit(solution)/shard_map/all_to_all | solution.py:263
  16.8 0.7 %shard_map.76 = bf16[8,64,128]{2,1,0:T(8,128)(2,1)S(1)} custom-call(bf16[512,1024]{1,0:T(8,128)(2,1)S(1)} %get-tuple-element.10.hi_ref, bf16[512,1024]{1,0:T(8,128)(2,1)S(1)} %get-tuple-element.11.lo_ref, bf16[16,64,128]{2,1,0:T(8,128)(2,1)S(1)} %all-to-all-done.hist_ref, bf16[32,2,32,128]{3,2,1,0:T(8,128)(2,1)S(1)} %copy-done.2), custom_call_target="tpu_custom_call" | custom-call | tf_op jit(solution)/shard_map/pallas_call | solution.py:284
  17.5 8.6 %all_to_all.15.recv_ref = bf16[8,64,128]{2,1,0:T(8,128)(2,1)S(1)} all-to-all(bf16[8,64,128]{2,1,0:T(8,128)(2,1)S(1)} %shard_map.76), channel_id=1, replica_groups={{0,16,32,48,64,80,96,112},{128,144,160,176,192,208,224,240},{1,17,33,49..., dimensions={0} | all-to-all | bytes 262144 | tf_op jit(solution)/shard_map/all_to_all | solution.py:285
  26.2 0.1 shard_map.77.own_ref.dens_ref
  26.3 1.1 %shard_map.79 = bf16[8,128,128]{2,1,0:T(8,128)(2,1)} custom-call(bf16[4,128,128]{2,1,0:T(8,128)(2,1)S(1)} %shard_map.77.own_ref.dens_ref, bf16[32,2,32,128]{3,2,1,0:T(8,128)(2,1)S(1)} %copy-done.2), custom_call_target="tpu_custom_call" | custom-call | tf_op jit(solution)/shard_map/pallas_call | solution.py:290
  27.4 8.2 %all-to-all-start.2 = ((bf16[8,128,128]{2,1,0:T(8,128)(2,1)}), bf16[8,128,128]{2,1,0:T(8,128)(2,1)S(1)}, u32[]{:S(2)}, u32[]{:S(2)}) async-start(bf16[8,128,128]{2,1,0:T(8,128)(2,1)} %shard_map.79), calls=%async_computation.2 | async-start | bytes 524288 | tf_op jit(solution)/shard_map/all_to_all | solution.py:291
  35.6 2.7 %collective-permute-start.3 = (bf16[4,128,128]{2,1,0:T(8,128)(2,1)S(1)}, bf16[4,128,128]{2,1,0:T(8,128)(2,1)S(1)}, u32[]{:S(2)}, u32[]{:S(2)}) collective-permute-start(bf16[4,128,128]{2,1,0:T(8,128)(2,1)S(1)} %shard_map.77.own_ref.dens_ref), channel_id=1, source_target_pairs={{2,0},{3,1},{4,2},{5,3},{6,4},{7,5},{8,6},{9,7},{10,8},{11,9},{12,... | collective-permute-start | bytes 393224 | tf_op jit(solution)/shard_map/ppermute | solution.py:37
  38.3 3.5 %collective-permute-start.1 = (bf16[4,128,128]{2,1,0:T(8,128)(2,1)S(1)}, bf16[4,128,128]{2,1,0:T(8,128)(2,1)S(1)}, u32[]{:S(2)}, u32[]{:S(2)}) collective-permute-start(bf16[4,128,128]{2,1,0:T(8,128)(2,1)S(1)} %shard_map.77.own_ref.dens_ref), channel_id=1, source_target_pairs={{0,1},{1,0},{2,3},{3,2},{4,5},{5,4},{6,7},{7,6},{8,9},{9,8},{10,11... | collective-permute-start | bytes 393224 | tf_op jit(solution)/shard_map/ppermute | solution.py:230
  41.8 2.1 %collective-permute-done.3.refs_2_ = bf16[4,128,128]{2,1,0:T(8,128)(2,1)S(1)} collective-permute-done((bf16[4,128,128]{2,1,0:T(8,128)(2,1)S(1)}, bf16[4,128,128]{2,1,0:T(8,128)(2,1)S(1)}, u32[]{:S(2)}, u32[]{:S(2)}) %collective-permute-start.3) | collective-permute-done | bytes 131104 | tf_op jit(solution)/shard_map/ppermute | solution.py:37
  43.8 3.5 %collective-permute-start.5 = (bf16[4,128,128]{2,1,0:T(8,128)(2,1)S(1)}, bf16[4,128,128]{2,1,0:T(8,128)(2,1)S(1)}, u32[]{:S(2)}, u32[]{:S(2)}) collective-permute-start(bf16[4,128,128]{2,1,0:T(8,128)(2,1)S(1)} %collective-permute-done.3.refs_2_), channel_id=1, source_target_pairs={{0,1},{1,0},{2,3},{3,2},{4,5},{5,4},{6,7},{7,6},{8,9},{9,8},{10,11... | collective-permute-start | bytes 393224 | tf_op jit(solution)/shard_map/ppermute | solution.py:230
  47.3 2.5 %collective-permute-start = (bf16[8,128,128]{2,1,0:T(8,128)(2,1)S(1)}, bf16[8,128,128]{2,1,0:T(8,128)(2,1)S(1)}, u32[]{:S(2)}, u32[]{:S(2)}) collective-permute-start(bf16[8,128,128]{2,1,0:T(8,128)(2,1)S(1)} %all-to-all-done.2.mine_ref), channel_id=1, source_target_pairs={{0,1},{1,0},{2,3},{3,2},{4,5},{5,4},{6,7},{7,6},{8,9},{9,8},{10,11... | collective-permute-start | bytes 786440 | tf_op jit(solution)/shard_map/ppermute | solution.py:230
  49.9 0.0 collective-permute-done.2.refs_1_
  49.9 0.3 collective-permute-start.6
  50.2 0.0 collective-permute-start.4
  50.2 3.5 %shard_map.78 = (f32[4,256,128]{2,1,0:T(8,128)S(1)}, bf16[3,32,2,128,128]{4,3,2,1,0:T(8,128)(2,1)S(1)}, bf16[4,128,512]{2,1,0:T(8,128)(2,1)S(1)}) custom-call(bf16[4,32,2,128,128]{4,3,2,1,0:T(8,128)(2,1)} %bitcast.8, bf16[4,128,128]{2,1,0:T(8,128)(2,1)S(1)} %shard_map.77.own_ref.dens_ref, bf16[32,2,32,128]{3,2,1,0:T(8,128)(2,1)S(1)} %copy-done.3), custom_call_target="tpu_custom_call" | custom-call | tf_op jit(solution)/shard_map/pallas_call | solution.py:293
  53.7 1.0 %collective-permute-done.6.refs_5_ = bf16[4,128,128]{2,1,0:T(8,128)(2,1)S(1)} collective-permute-done((bf16[4,128,128]{2,1,0:T(8,128)(2,1)S(1)}, bf16[4,128,128]{2,1,0:T(8,128)(2,1)S(1)}, u32[]{:S(2)}, u32[]{:S(2)}) %collective-permute-start.6) | collective-permute-done | bytes 131104 | tf_op jit(solution)/shard_map/ppermute | solution.py:235
  54.7 4.1 %shard_map.80 = bf16[32,16,128]{2,1,0:T(8,128)(2,1)} custom-call(s32[6]{0:T(128)S(1)} %pad_add_fusion.info_ref, bf16[3,32,2,128,128]{4,3,2,1,0:T(8,128)(2,1)S(1)} %get-tuple-element.12.blocks_ref, f32[4,256,128]{2,1,0:T(8,128)S(1)} %get-tuple-element.13.first_ref, bf16[8,128,128]{2,1,0:T(8,128)(2,1)S(1)} %all-to-all-done.2.mine_ref, ...), custom_call_target="tpu_custom_call" | custom-call | tf_op jit(solution)/shard_map/pallas_call | solution.py:301
  (16 shorter events, 0.0 us)
Async XLA Ops:
  0.0 9.4 %copy-start = (s32[16,4]{0,1:T(4,128)S(1)}, s32[16,4]{0,1:T(4,128)}, u32[]{:S(2)}) copy-start(s32[16,4]{0,1:T(4,128)} %param.9) | copy-start | bytes 772
  0.0 16.8 %copy-start.2 = (bf16[32,2,32,128]{3,2,1,0:T(8,128)(2,1)S(1)}, bf16[32,2,32,128]{3,2,1,0:T(8,128)(2,1)}, u32[]{:S(2)}) copy-start(bf16[32,2,32,128]{3,2,1,0:T(8,128)(2,1)} %basis_ref.5) | copy-start | bytes 1572868
  0.0 50.2 %copy-start.3 = (bf16[32,2,32,128]{3,2,1,0:T(8,128)(2,1)S(1)}, bf16[32,2,32,128]{3,2,1,0:T(8,128)(2,1)}, u32[]{:S(2)}) copy-start(bf16[32,2,32,128]{3,2,1,0:T(8,128)(2,1)} %basis_ref.4) | copy-start | bytes 1572868
  0.0 1.0 %copy-start.4 = (bf16[64,8,128]{2,1,0:T(8,128)(2,1)S(1)}, bf16[64,8,128]{2,1,0:T(8,128)(2,1)}, u32[]{:S(2)}) copy-start(bf16[64,8,128]{2,1,0:T(8,128)(2,1)} %hist_ref.1) | copy-start | bytes 393220
  1.8 15.0 %all-to-all-start = ((bf16[16,64,128]{2,1,0:T(8,128)(2,1)}), bf16[16,64,128]{2,1,0:T(8,128)(2,1)S(1)}, u32[]{:S(2)}, u32[]{:S(2)}) async-start(bf16[16,64,128]{2,1,0:T(8,128)(2,1)} %shard_map.75), calls=%async_computation | async-start | bytes 524288 | tf_op jit(solution)/shard_map/all_to_all | solution.py:263
  17.5 37.1 %copy-start.1 = (bf16[32,2,32,512]{3,2,1,0:T(8,128)(2,1)S(1)}, bf16[32,2,32,512]{3,2,1,0:T(8,128)(2,1)}, u32[]{:S(2)}) copy-start(bf16[32,2,32,512]{3,2,1,0:T(8,128)(2,1)} %shard_map.73.masked_hbm.couple_ref) | copy-start | bytes 6291460
  27.4 19.9 %all-to-all-start.2 = ((bf16[8,128,128]{2,1,0:T(8,128)(2,1)}), bf16[8,128,128]{2,1,0:T(8,128)(2,1)S(1)}, u32[]{:S(2)}, u32[]{:S(2)}) async-start(bf16[8,128,128]{2,1,0:T(8,128)(2,1)} %shard_map.79), calls=%async_computation.2 | async-start | bytes 524288 | tf_op jit(solution)/shard_map/all_to_all | solution.py:291
  35.6 8.3 %collective-permute-start.3 = (bf16[4,128,128]{2,1,0:T(8,128)(2,1)S(1)}, bf16[4,128,128]{2,1,0:T(8,128)(2,1)S(1)}, u32[]{:S(2)}, u32[]{:S(2)}) collective-permute-start(bf16[4,128,128]{2,1,0:T(8,128)(2,1)S(1)} %shard_map.77.own_ref.dens_ref), channel_id=1, source_target_pairs={{2,0},{3,1},{4,2},{5,3},{6,4},{7,5},{8,6},{9,7},{10,8},{11,9},{12,... | collective-permute-start | bytes 393224 | tf_op jit(solution)/shard_map/ppermute | solution.py:37
  38.2 11.6 %collective-permute-start.2 = (bf16[4,128,128]{2,1,0:T(8,128)(2,1)S(1)}, bf16[4,128,128]{2,1,0:T(8,128)(2,1)S(1)}, u32[]{:S(2)}, u32[]{:S(2)}) collective-permute-start(bf16[4,128,128]{2,1,0:T(8,128)(2,1)S(1)} %shard_map.77.own_ref.dens_ref), channel_id=1, source_target_pairs={{14,0},{15,1},{0,2},{1,3},{2,4},{3,5},{4,6},{5,7},{6,8},{7,9},{8,1... | collective-permute-start | bytes 393224 | tf_op jit(solution)/shard_map/ppermute | solution.py:37
  38.3 15.4 %collective-permute-start.1 = (bf16[4,128,128]{2,1,0:T(8,128)(2,1)S(1)}, bf16[4,128,128]{2,1,0:T(8,128)(2,1)S(1)}, u32[]{:S(2)}, u32[]{:S(2)}) collective-permute-start(bf16[4,128,128]{2,1,0:T(8,128)(2,1)S(1)} %shard_map.77.own_ref.dens_ref), channel_id=1, source_target_pairs={{0,1},{1,0},{2,3},{3,2},{4,5},{5,4},{6,7},{7,6},{8,9},{9,8},{10,11... | collective-permute-start | bytes 393224 | tf_op jit(solution)/shard_map/ppermute | solution.py:230
  43.8 9.8 %collective-permute-start.5 = (bf16[4,128,128]{2,1,0:T(8,128)(2,1)S(1)}, bf16[4,128,128]{2,1,0:T(8,128)(2,1)S(1)}, u32[]{:S(2)}, u32[]{:S(2)}) collective-permute-start(bf16[4,128,128]{2,1,0:T(8,128)(2,1)S(1)} %collective-permute-done.3.refs_2_), channel_id=1, source_target_pairs={{0,1},{1,0},{2,3},{3,2},{4,5},{5,4},{6,7},{7,6},{8,9},{9,8},{10,11... | collective-permute-start | bytes 393224 | tf_op jit(solution)/shard_map/ppermute | solution.py:230
  47.3 7.3 %collective-permute-start = (bf16[8,128,128]{2,1,0:T(8,128)(2,1)S(1)}, bf16[8,128,128]{2,1,0:T(8,128)(2,1)S(1)}, u32[]{:S(2)}, u32[]{:S(2)}) collective-permute-start(bf16[8,128,128]{2,1,0:T(8,128)(2,1)S(1)} %all-to-all-done.2.mine_ref), channel_id=1, source_target_pairs={{0,1},{1,0},{2,3},{3,2},{4,5},{5,4},{6,7},{7,6},{8,9},{9,8},{10,11... | collective-permute-start | bytes 786440 | tf_op jit(solution)/shard_map/ppermute | solution.py:230
  49.9 4.8 %collective-permute-start.6 = (bf16[4,128,128]{2,1,0:T(8,128)(2,1)S(1)}, bf16[4,128,128]{2,1,0:T(8,128)(2,1)S(1)}, u32[]{:S(2)}, u32[]{:S(2)}) collective-permute-start(bf16[4,128,128]{2,1,0:T(8,128)(2,1)S(1)} %broadcast_select_fusion), channel_id=1, source_target_pairs={{0,15},{1,2},{2,1},{3,4},{4,3},{5,6},{6,5},{7,8},{8,7},{9,10},{10,... | collective-permute-start | bytes 393224 | tf_op jit(solution)/shard_map/ppermute | solution.py:235
  50.2 4.5 %collective-permute-start.4 = (bf16[4,128,128]{2,1,0:T(8,128)(2,1)S(1)}, bf16[4,128,128]{2,1,0:T(8,128)(2,1)S(1)}, u32[]{:S(2)}, u32[]{:S(2)}) collective-permute-start(bf16[4,128,128]{2,1,0:T(8,128)(2,1)S(1)} %collective-permute-done.2.refs_1_), channel_id=1, source_target_pairs={{0,1},{1,0},{2,3},{3,2},{4,5},{5,4},{6,7},{7,6},{8,9},{9,8},{10,11... | collective-permute-start | bytes 393224 | tf_op jit(solution)/shard_map/ppermute | solution.py:230
